TPU v7x, 32 devices: a whole 2x2x4 slice. The times are simulated.
32 devices in a mesh: depth: 16 (over z, x, core), azi: 2 (over y).
Axes of the slice: x: 2, y: 2, z: 4, core: 2. Of those that a mesh axis runs over, the one named last changes fastest.
Arguments:
- heat_state: float32 [256, 128, 1024], P('depth', None, 'azi'), may hold values from -6 to 6
- tangent_in: float32 [256, 128, 1024], P('depth', None, 'azi'), may hold values from -6 to 6
- cotangent: float32 [256, 128, 1024], P('depth', None, 'azi'), may hold values from -6 to 6
- wet_mask: int32 [256, 1024], P('depth', 'azi'), may hold values 0 or 1
- sensors: int32 [256, 1024], P('depth', 'azi'), may hold values from 0 to 127
- propagators: bfloat16 [1024, 128, 128], P('azi', 'depth'), as said below
Outputs:
- new_state: bfloat16 [256, 128, 1024], P('depth', None, 'azi')
- tangent_out: bfloat16 [256, 128, 1024], P('depth', None, 'azi')
- gradient: float32 [256, 128, 1024], P('depth', None, 'azi')
- readings: bfloat16 [256, 1024], P('depth', 'azi')
Inputs may be any that keep to these rules, and one draw needn't show every extreme that they name: `propagators`: each mode's radial propagator has diagonal entries between 0.55 and 1 and off-diagonal entries of magnitude at most 1.4 / sqrt(128).
All inputs are finite; a program needn't handle non-finite values. No bound on the sum of `wet_mask` on one device may be relied on, other than what follows from the above.
Results may differ from a plain program's by a relative error of at most 0.0078.
Values may be sent and summed in bfloat16 or wider, within the bound.
A program may use at most 128 MiB of HBM per device.

v0:
```python
import functools
import math

import jax
import jax.numpy as jnp
import numpy as np
from jax import lax
from jax.experimental import pallas as pl
from jax.experimental.pallas import tpu as pltpu
from jax.sharding import PartitionSpec as P

mixing = 0.25
evaporation = 0.6
skin_depth = 16.0
mode_chunks = 2


def halo_planes(last, first):
    size = lax.axis_size("depth")
    up = [(i, i + 1) for i in range(size - 1)]
    down = [(j, i) for i, j in up]
    before = lax.ppermute(last, "depth", up)
    after = lax.ppermute(first, "depth", down)
    return before, after


def damping_profile(rows, lanes):
    radius = pl.program_id(0) * rows + lax.broadcasted_iota(jnp.int32, (rows, lanes), 0)
    return evaporation * jnp.exp(-radius.astype(jnp.float32) / skin_depth)


def plane(ref, before, after, z):
    source, index = (before, 0) if z < 0 else (after, 0) if z == ref.shape[0] else (ref, z)
    return source[index].astype(jnp.float32)


def mixed(ref, before, after, z):
    centre = plane(ref, before, after, z)
    around = plane(ref, before, after, z + 1) + plane(ref, before, after, z - 1)
    return centre, centre + mixing * (around - 2.0 * centre)


def rhs_kernel(wet, heat, heat_before, heat_after, tangent, tangent_before, tangent_after, out, tangent_out):
    slab, rows, lanes = heat.shape
    profile = damping_profile(rows, lanes)
    for z in range(slab):
        damping = wet[z : z + 1].astype(jnp.float32) * profile
        centre, value = mixed(heat, heat_before, heat_after, z)
        moisture = jnp.tanh(centre)
        out[z] = (value - damping * moisture).astype(out.dtype)
        slope = 1.0 - moisture * moisture
        centre, value = mixed(tangent, tangent_before, tangent_after, z)
        tangent_out[z] = (value - damping * slope * centre).astype(tangent_out.dtype)


def gradient_kernel(wet, heat, dual, dual_before, dual_after, out):
    slab, rows, lanes = heat.shape
    profile = damping_profile(rows, lanes)
    for z in range(slab):
        damping = wet[z : z + 1].astype(jnp.float32) * profile
        moisture = jnp.tanh(heat[z])
        slope = 1.0 - moisture * moisture
        centre, value = mixed(dual, dual_before, dual_after, z)
        out[z] = value - damping * slope * centre


def by_radius(kernel, wet, fields, dtypes):
    slab, radial, lanes = fields[0].shape
    rows = min(radial, 16)

    def spec(depth):
        return pl.BlockSpec((depth, rows, lanes), lambda i: (0, i, 0))

    count = len(dtypes) * slab * radial * lanes
    return pl.pallas_call(
        kernel,
        grid=(radial // rows,),
        in_specs=[pl.BlockSpec(wet.shape, lambda i: (0, 0))] + [spec(f.shape[0]) for f in fields],
        out_specs=[spec(slab) for _ in dtypes],
        out_shape=[jax.ShapeDtypeStruct((slab, radial, lanes), dtype) for dtype in dtypes],
        cost_estimate=pl.CostEstimate(flops=10 * count, bytes_accessed=6 * count, transcendentals=count),
    )(wet, *fields)


def fourier_table(length):
    wavenumber = np.arange(length, dtype=np.int32)[:, None]
    position = np.arange(length, dtype=np.int32)[None, :]
    midpoint = length // 2
    harmonic = np.where(wavenumber <= midpoint, wavenumber, wavenumber - midpoint)
    phase = (harmonic * position % length).astype(np.float32) * np.float32(2.0 * math.pi / length)
    waveform = np.where(wavenumber <= midpoint, np.cos(phase), np.sin(phase))
    boundary = (wavenumber == 0) | (wavenumber == midpoint)
    weights = np.where(boundary, math.sqrt(1.0 / length), math.sqrt(2.0 / length)).astype(np.float32)
    return (waveform * weights).astype(jnp.bfloat16)


def from_all(value):
    size = lax.axis_size("azi")
    blocks = [value]
    for shift in range(1, size):
        pairs = [(i, (i + shift) % size) for i in range(size)]
        blocks.append(lax.ppermute(value, "azi", pairs))
    return blocks


def split_body(table, heat_state, tangent_in, cotangent, wet_mask, sensors, propagators):
    slab, radial, local_azi = heat_state.shape
    size = lax.axis_size("azi")
    me = lax.axis_index("azi")
    owners = [lax.rem(me - shift + size, size) for shift in range(size)]
    modes = propagators.shape[0]
    step = modes // mode_chunks

    whole = [
        lax.all_gather(propagators[c * step : (c + 1) * step], "depth", axis=1, tiled=True)
        for c in range(mode_chunks)
    ]

    own_modes = lax.dynamic_slice_in_dim(table, me * modes, modes, axis=0)
    to_modes = [
        lax.dynamic_slice_in_dim(own_modes, owner * local_azi, local_azi, axis=1) for owner in owners
    ]
    own_azimuths = lax.dynamic_slice_in_dim(table, me * local_azi, local_azi, axis=1)
    to_azimuths = [
        lax.dynamic_slice_in_dim(own_azimuths, owner * modes, modes, axis=0) for owner in owners
    ]

    def part_spectrum(weights, block, c):
        return jnp.einsum(
            "ka,zra->kzr",
            weights[c * step : (c + 1) * step],
            block,
            preferred_element_type=jnp.float32,
        )

    seed_blocks = from_all(cotangent.astype(jnp.bfloat16))
    seed_part, heat_last, heat_first, tangent_last, tangent_first = lax.optimization_barrier(
        (
            part_spectrum(to_modes[0], seed_blocks[0], 0),
            heat_state[-1:],
            heat_state[:1],
            tangent_in[-1:],
            tangent_in[:1],
        )
    )

    forward_rhs, tangent_rhs = by_radius(
        rhs_kernel,
        wet_mask,
        [heat_state, *halo_planes(heat_last, heat_first), tangent_in, *halo_planes(tangent_last, tangent_first)],
        [jnp.bfloat16] * 2,
    )
    own_seed, forward_rhs, tangent_rhs = lax.optimization_barrier(
        (seed_blocks[0], forward_rhs, tangent_rhs)
    )
    seed_blocks = [own_seed] + seed_blocks[1:]
    forward_blocks = from_all(forward_rhs)
    tangent_blocks = from_all(tangent_rhs)

    def solve(blocks, formula, first=None):
        returned = []
        for c in range(mode_chunks):
            known = c == 0 and first is not None
            total = first if known else part_spectrum(to_modes[0], blocks[0], c)
            for weights, block in zip(to_modes[1:], blocks[1:]):
                total = total + part_spectrum(weights, block, c)
            solved = jnp.einsum(
                formula, whole[c], total.astype(jnp.bfloat16), preferred_element_type=jnp.float32
            ).astype(jnp.bfloat16)
            returned.append(from_all(solved))
        return returned

    def part_inverse(returned, pairs):
        total = 0.0
        for c, i in pairs:
            total = total + jnp.einsum(
                "ka,kzr->zra",
                to_azimuths[i][c * step : (c + 1) * step],
                returned[c][i],
                preferred_element_type=jnp.float32,
            )
        return total

    pairs = [(c, i) for i in range(size) for c in range(mode_chunks)]

    def inverse(returned):
        return part_inverse(returned, pairs).astype(jnp.bfloat16)

    dual_modes = solve(seed_blocks, "ksr,kzs->kzr", seed_part)
    dual_modes[0][0], *forward_received = lax.optimization_barrier(
        (dual_modes[0][0], *forward_blocks[1:])
    )
    forward_blocks = forward_blocks[:1] + forward_received
    forward_modes = solve(forward_blocks, "krs,kzs->kzr")
    tangent_modes = solve(tangent_blocks, "krs,kzs->kzr")

    dual = inverse(dual_modes)
    (gradient,) = by_radius(
        gradient_kernel, wet_mask, [heat_state, dual, *halo_planes(dual[-1:], dual[:1])], [jnp.float32]
    )

    new_state = inverse(forward_modes)
    radial_index = jnp.arange(radial, dtype=jnp.int32)[None, :, None]
    selected = jnp.where(radial_index == sensors[:, None, :], new_state, jnp.zeros_like(new_state))
    readings = jnp.sum(selected, axis=1)

    partial = part_inverse(tangent_modes, pairs[:-1])
    gradient, partial, tangent_modes[-1][-1] = lax.optimization_barrier(
        (gradient, partial, tangent_modes[-1][-1])
    )
    tangent_out = (partial + part_inverse(tangent_modes, pairs[-1:])).astype(jnp.bfloat16)
    return (new_state, tangent_out, gradient, readings)


fields = 3
blocks = 8
early = blocks // 2
own, other = 0, 1


def line_order():
    first = [(q, own, p) for p in range(3) for q in range(early)]
    later = [(q, own) for q in range(early, blocks)] + [(blocks - 1, other)]
    return first + [(q, c, p) for p in range(3) for q, c in later]


def pair_order():
    first = [(q, s) for s in range(4) for q in range(early)]
    first.insert(10, (blocks - 1, 0))
    return first + [(q, s) for s in range(4) for q in range(early, blocks - 1)]


def modes_kernel(
    shard, weights, seed, forward, tangent,
    out_seed, out_forward, out_tangent,
    matrices, table, values, stage, mine, theirs, given,
    pair_send, pair_recv, up_send, up_recv, down_send, down_recv, azi_send, azi_recv,
    twin_send, twin_recv, back_send, back_recv, keep_sem, load_sem,
):
    sources, outs = (seed, forward, tangent), (out_seed, out_forward, out_tangent)
    flips = (True, False, False)
    place, azi = lax.axis_index("depth"), lax.axis_index("azi")
    z, x, core = place // 4, place // 2 % 2, place % 2
    pair, twin, up, down = place + 2 - 4 * x, place + 1 - 2 * core, place + 4, place - 4
    count, radial, _ = matrices.shape
    step = count // blocks
    half = count // 2
    rows = shard.shape[1]
    slab = mine.shape[2]
    local = seed.shape[1]
    planes = slab // blocks
    mesh_ids = pl.DeviceIdType.MESH

    barrier = pltpu.get_barrier_semaphore()

    def greet(where, azimuth):
        pl.semaphore_signal(barrier, inc=1, device_id=(where, azimuth), device_id_type=mesh_ids)

    greet(pair, azi)
    greet(twin, azi)
    greet(place, 1 - azi)

    @pl.when(z < 3)
    def _():
        greet(up, azi)

    @pl.when(z > 0)
    def _():
        greet(down, azi)

    pl.semaphore_wait(barrier, 4 + (z + 1) // 2 % 2)

    def remote(src, dst, send, recv, where, azimuth=azi):
        return pltpu.make_async_remote_copy(
            src_ref=src, dst_ref=dst, send_sem=send, recv_sem=recv,
            device_id=(where, azimuth), device_id_type=mesh_ids,
        )

    def region(q, line, side):
        at = pl.multiple_of(rows * (2 * line + side), rows)
        return matrices.at[pl.ds(q * step, step), pl.ds(at, rows), :]

    flipped = (z, z + 1 - 2 * (z % 2), z + 2 - 4 * (z // 2), 3 - z)

    def pair_copy(q, s):
        ref = region(q, flipped[s], x)
        return remote(ref, ref, pair_send.at[q, s], pair_recv.at[q, s], pair)

    def line_item(q, c):
        return blocks if c == other else q

    def up_copy(q, c, p):
        ref = region(q, z - p, x if c == own else 1 - x)
        k = line_item(q, c)
        return remote(ref, ref, up_send.at[k, p], up_recv.at[k, p], up)

    def down_copy(q, c, p):
        ref = region(q, z + p, x if c == own else 1 - x)
        k = line_item(q, c)
        return remote(ref, ref, down_send.at[k, p], down_recv.at[k, p], down)

    def azi_copy(n):
        if n < early:
            return remote(
                region(n, z, x), region(n + early, z, x), azi_send.at[n], azi_recv.at[n], place, 1 - azi
            )
        f, part = divmod(n - early, blocks)
        span = planes * radial
        at = pl.ds(part * span, span)
        return remote(
            values.at[f, at, pl.ds(0, local)],
            values.at[f, at, pl.ds(local, local)],
            azi_send.at[n], azi_recv.at[n], place, 1 - azi,
        )

    pairs, lines, azis = pair_order(), line_order(), early + fields * blocks

    def send(t):
        if t < len(pairs):
            pair_copy(*pairs[t]).start()
        if t < azis:
            azi_copy(t).start()
        if t < len(lines):
            q, c, p = lines[t]

            @pl.when((z < 3) & (z >= p))
            def _():
                up_copy(q, c, p).start()

            @pl.when((z > 0) & (z + p <= 3))
            def _():
                down_copy(q, c, p).start()

    def receive(t):
        if 0 <= t < len(pairs):
            pair_copy(*pairs[t]).wait_recv()
        if 0 <= t < azis:
            azi_copy(t).wait_recv()
        if 0 <= t < len(lines):
            q, c, p = lines[t]

            @pl.when(z >= p + 1)
            def _():
                up_copy(q, c, p).wait_recv()

            @pl.when(z + p + 1 <= 3)
            def _():
                down_copy(q, c, p).wait_recv()

    def sent(t):
        if t < len(pairs):
            pair_copy(*pairs[t]).wait_send()
        if t < azis:
            azi_copy(t).wait_send()
        if t < len(lines):
            q, c, p = lines[t]

            @pl.when((z < 3) & (z >= p))
            def _():
                up_copy(q, c, p).wait_send()

            @pl.when((z > 0) & (z + p <= 3))
            def _():
                down_copy(q, c, p).wait_send()

    at = pl.multiple_of(rows * (2 * z + x), rows)
    loads = [pltpu.make_async_copy(shard, matrices.at[pl.ds(0, half), pl.ds(at, rows), :], load_sem.at[0])]
    for f in range(fields):
        loads.append(
            pltpu.make_async_copy(sources[f], values.at[f, :, pl.ds(0, local)], load_sem.at[1 + f])
        )
    loads.append(pltpu.make_async_copy(weights, table, load_sem.at[1 + fields]))
    for load in loads:
        load.start()
    for load in loads:
        load.wait()

    def twin_copy(f, part):
        at = pl.ds(part * half, half)
        return remote(
            given.at[f, at], theirs.at[f, at], twin_send.at[f, part], twin_recv.at[f, part], twin
        )

    def transform(f, part):
        into, first = (given, part) if part < 2 else (mine, part - 2)

        def planes_step(n, _):
            cols = values[f, pl.ds(pl.multiple_of(n * 2 * radial, 2 * radial), 2 * radial), :]
            out = lax.dot_general(
                table[pl.ds(part * half, half), :], cols, (((1,), (1,)), ((), ())),
                preferred_element_type=jnp.float32,
            )
            stage[pl.ds(pl.multiple_of(n * 2 * half, half), half), :] = out[:, :radial]
            stage[pl.ds(pl.multiple_of(n * 2 * half + half, half), half), :] = out[:, radial:]
            return 0

        lax.fori_loop(0, slab // 2, planes_step, 0)

        def turn(n, _):
            for u in range(8):
                k = n * 8 + u
                into[f, first * half + k] = stage[pl.ds(k, slab, stride=half), :].astype(jnp.bfloat16)
            return 0

        lax.fori_loop(0, half // 8, turn, 0)
        if part < 2:
            twin_copy(f, part).start()

    def keep_copy(f, q):
        at = pl.ds(q * step, step)
        return pltpu.make_async_copy(mine.at[f, at], outs[f].at[at], keep_sem.at[f, q])

    def back_copy(f, q):
        return remote(
            theirs.at[f, pl.ds(q * step, step)],
            outs[f].at[pl.ds(count + q * step, step)],
            back_send.at[f, q], back_recv.at[f, q], twin,
        )

    def solve(which, q):
        def one(n, _):
            for u in range(4):
                k = q * step + n * 4 + u
                matrix = matrices[k]
                for flip in (True, False):
                    chosen = [f for f in which if flips[f] == flip]
                    if not chosen:
                        continue
                    stacked = jnp.concatenate(
                        [part[f, k] for f in chosen for part in (mine, theirs)], axis=0
                    )
                    out = lax.dot_general(
                        stacked, matrix, (((1,), (0 if flip else 1,)), ((), ())),
                        preferred_element_type=jnp.float32,
                    ).astype(jnp.bfloat16)
                    for i, f in enumerate(chosen):
                        mine[f, k] = out[2 * i * slab : (2 * i + 1) * slab]
                        theirs[f, k] = out[(2 * i + 1) * slab : (2 * i + 2) * slab]
            return 0

        lax.fori_loop(0, step // 4, one, 0)
        for f in which:
            keep_copy(f, q).start()
            back_copy(f, q).start()

    def met(f):
        for part in range(2):
            twin_copy(f, part).wait_recv()

    tasks = {
        13: [lambda: transform(0, 0), lambda: transform(0, 1)],
        14: [lambda: transform(0, 2), lambda: transform(0, 3)],
        16: [lambda: met(0), lambda: solve([0], 0)],
        17: [lambda: solve([0], 1), lambda: solve([0], 2)],
        18: [lambda: solve([0], 3)],
        21: [lambda: transform(1, 0), lambda: transform(1, 1)],
        22: [lambda: transform(1, 2), lambda: transform(1, 3)],
        24: [lambda: met(1), lambda: solve([1], 0), lambda: solve([1], 1)],
        25: [lambda: solve([1], 2)],
        26: [lambda: solve([1], 3)],
        29: [functools.partial(transform, 2, part) for part in range(4)]
        + [lambda: solve([0, 1], 4)],
        30: [lambda: solve([0, 1], 7), lambda: solve([0, 1], 5), lambda: met(2)]
        + [functools.partial(solve, [2], q) for q in (0, 1, 2, 3, 4, 7, 5)],
        31: [lambda: solve([0, 1, 2], 6)],
    }

    lag = 2
    for t in range(32):
        receive(t - lag)
        send(t)
        for task in tasks.get(t, []):
            task()

    for t in range(32):
        sent(t)
    for f in range(fields):
        for part in range(2):
            twin_copy(f, part).wait_send()
        for q in range(blocks):
            keep_copy(f, q).wait()
            back_copy(f, q).wait()


def solved_modes(shard, weights, seed, forward, tangent):
    slab, radial, local = seed.shape
    half, rows, _ = shard.shape
    count = 2 * half
    dma = pltpu.SemaphoreType.DMA
    flat = [v.reshape(slab * radial, local) for v in (seed, forward, tangent)]
    out = jax.ShapeDtypeStruct((2 * count, slab, radial), jnp.bfloat16)
    return pl.pallas_call(
        modes_kernel,
        out_shape=[out] * fields,
        in_specs=[pl.BlockSpec(memory_space=pl.ANY)] * 5,
        out_specs=[pl.BlockSpec(memory_space=pl.ANY)] * fields,
        scratch_shapes=[
            pltpu.VMEM((count, radial, radial), jnp.bfloat16),
            pltpu.VMEM((2 * count, 2 * local), jnp.bfloat16),
            pltpu.VMEM((fields, slab * radial, 2 * local), jnp.bfloat16),
            pltpu.VMEM((slab * half, radial), jnp.float32),
            pltpu.VMEM((fields, count, slab, radial), jnp.bfloat16),
            pltpu.VMEM((fields, count, slab, radial), jnp.bfloat16),
            pltpu.VMEM((fields, count, slab, radial), jnp.bfloat16),
            dma((blocks, 4)), dma((blocks, 4)),
            dma((blocks + 1, 3)), dma((blocks + 1, 3)),
            dma((blocks + 1, 3)), dma((blocks + 1, 3)),
            dma((early + fields * blocks,)), dma((early + fields * blocks,)),
            dma((fields, 2)), dma((fields, 2)),
            dma((fields, blocks)), dma((fields, blocks)), dma((fields, blocks)),
            dma((fields + 2,)),
        ],
        compiler_params=pltpu.CompilerParams(
            collective_id=0, has_side_effects=True, vmem_limit_bytes=58 * 1024 * 1024
        ),
        cost_estimate=pl.CostEstimate(flops=15 * 10**9, bytes_accessed=10**8, transcendentals=0),
    )(shard, weights, *flat)


def fused_body(table, heat_state, tangent_in, cotangent, wet_mask, sensors, propagators):
    slab, radial, local_azi = heat_state.shape
    depth = lax.axis_size("depth")
    me = lax.axis_index("azi")
    core = lax.rem(lax.axis_index("depth"), 2)
    modes = propagators.shape[0]
    half = modes // 2

    mine = lax.dynamic_slice_in_dim(propagators, core * half, half, axis=0)
    outgoing = lax.dynamic_slice_in_dim(propagators, (1 - core) * half, half, axis=0)
    incoming = lax.ppermute(outgoing, "depth", [(i, i ^ 1) for i in range(depth)])
    shard = jnp.concatenate(
        [jnp.where(core == 0, mine, incoming), jnp.where(core == 0, incoming, mine)], axis=1
    )

    def table_rows(which):
        return [
            lax.dynamic_slice_in_dim(table, owner * modes + which * half, half, axis=0)
            for owner in (me, 1 - me)
        ]

    own_rows = jnp.concatenate(table_rows(core), axis=0)
    twin_rows = jnp.concatenate(table_rows(1 - core), axis=0)

    def columns(weights, owner):
        return lax.dynamic_slice_in_dim(weights, owner * local_azi, local_azi, axis=1)

    weights = jnp.concatenate([twin_rows, own_rows], axis=0)
    weights = jnp.concatenate([columns(weights, me), columns(weights, 1 - me)], axis=1)
    to_azimuths = columns(jnp.concatenate([own_rows, twin_rows], axis=0), me)

    forward_rhs, tangent_rhs = by_radius(
        rhs_kernel,
        wet_mask,
        [
            heat_state,
            *halo_planes(heat_state[-1:], heat_state[:1]),
            tangent_in,
            *halo_planes(tangent_in[-1:], tangent_in[:1]),
        ],
        [jnp.bfloat16] * 2,
    )
    dual_modes, forward_modes, tangent_modes = solved_modes(
        shard, weights, cotangent.astype(jnp.bfloat16), forward_rhs, tangent_rhs
    )

    def inverse(solved):
        return jnp.einsum(
            "ka,kzr->zra", to_azimuths, solved, preferred_element_type=jnp.float32
        ).astype(jnp.bfloat16)

    dual = inverse(dual_modes)
    (gradient,) = by_radius(
        gradient_kernel, wet_mask, [heat_state, dual, *halo_planes(dual[-1:], dual[:1])], [jnp.float32]
    )
    new_state = inverse(forward_modes)
    radial_index = jnp.arange(radial, dtype=jnp.int32)[None, :, None]
    selected = jnp.where(radial_index == sensors[:, None, :], new_state, jnp.zeros_like(new_state))
    readings = jnp.sum(selected, axis=1)
    tangent_out = inverse(tangent_modes)
    return (new_state, tangent_out, gradient, readings)


def solution(mesh):
    def run(heat_state, tangent_in, cotangent, wet_mask, sensors, propagators):
        table = jnp.asarray(fourier_table(heat_state.shape[2]))
        field = P("depth", None, "azi")
        fits = mesh.shape["azi"] == 2 and mesh.shape["depth"] == 16
        body = fused_body if fits else split_body
        panel = P("depth", "azi")
        return jax.shard_map(
            body,
            mesh=mesh,
            in_specs=(P(), field, field, field, panel, panel, P("azi", "depth", None)),
            out_specs=(field, field, field, panel),
            check_vma=False,
        )(table, heat_state, tangent_in, cotangent, wet_mask, sensors, propagators)

    return run
```

profile of v0, /device:TPU:1, one launch (start us, length us, event | category | flops | bytes accessed | tf_op | source)
XLA Modules:
  0.0 295.1 jit_solution(10405140764614635589)
XLA Ops:
  0.6 0.0 copy-start.5
  0.6 2.0 fusion.21
  2.7 2.0 collective-permute-start.4
  4.6 4.5 %collective-permute-start.3 = (f32[1,128,512]{2,1,0:T(8,128)}, f32[1,128,512]{2,1,0:T(8,128)}, u32[]{:S(2)}, u32[]{:S(2)}) collective-permute-start(f32[1,128,512]{2,1,0:T(8,128)} %get-tuple-element.15), channel_id=1, source_target_pairs={{0,2},{2,4},{4,6},{6,8},{8,10},{10,12},{12,14},{14,16},{16,18},{18... | collective-permute-start | bytes 786440 | tf_op jit(solution)/shard_map/ppermute | solution.py:22
  9.1 1.9 fusion.22
  11.0 1.9 collective-permute-start.2
  12.9 3.6 %collective-permute-start.1 = (f32[1,128,512]{2,1,0:T(8,128)}, f32[1,128,512]{2,1,0:T(8,128)}, u32[]{:S(2)}, u32[]{:S(2)}) collective-permute-start(f32[1,128,512]{2,1,0:T(8,128)} %get-tuple-element.17), channel_id=1, source_target_pairs={{0,2},{2,4},{4,6},{6,8},{8,10},{10,12},{12,14},{14,16},{16,18},{18... | collective-permute-start | bytes 786440 | tf_op jit(solution)/shard_map/ppermute | solution.py:22
  16.6 1.9 constant_dynamic-slice_fusion.6
  18.4 0.0 collective-permute-start
  18.4 0.0 copy-done.5
  18.4 0.2 constant_dynamic-slice_fusion.4
  18.7 0.0 copy-start
  18.7 0.0 copy-start.2
  18.7 0.8 copy-done
  19.5 0.2 copy-done.2
  19.7 0.2 pad_maximum_fusion
  19.9 3.8 %convert_element_type.14 = bf16[16,128,512]{2,1,0:T(8,128)(2,1)} convert(f32[16,128,512]{2,1,0:T(8,128)} %param.9) | non-fusion elementwise | flops 1048576 | bytes 6291456 | tf_op jit(solution)/shard_map/convert_element_type | solution.py:563
  23.7 0.0 copy-start.1
  23.7 0.0 copy-start.3
  23.7 0.2 constant_dynamic-slice_fusion.1
  23.9 0.8 copy-done.1
  24.7 0.2 copy-done.3
  24.9 0.1 fusion.20
  25.0 1.6 pad_maximum_fusion.1.weights
  26.5 0.0 copy-start.6
  26.5 0.0 collective-permute-done.4.tangent_after
  26.6 0.0 copy-start.7
  26.6 0.0 collective-permute-done.3.tangent_before
  26.6 0.0 collective-permute-done.2.heat_after
  26.6 0.0 collective-permute-done.1.heat_before
  26.6 0.7 copy-done.7
  27.3 8.9 %shard_map.102 = (bf16[16,128,512]{2,1,0:T(8,128)(2,1)}, bf16[16,128,512]{2,1,0:T(8,128)(2,1)}) custom-call(s32[16,512]{1,0:T(8,128)} %wet.3, f32[16,128,512]{2,1,0:T(8,128)} %heat.3, f32[1,128,512]{2,1,0:T(8,128)} %collective-permute-done.1.heat_before, f32[1,128,512]{2,1,0:T(8,128)} %collective-permute-done.2.heat_after, f32[16,128,512]{2,1,0:T(8,128)} %tangent.1, ...), custom_call_target="tpu_custom_call" | custom-call | flops 20971520 | bytes 12582912 | tf_op jit(solution)/shard_map/pallas_call | solution.py:75
  36.2 0.0 collective-permute-done
  36.2 0.0 copy-done.6
  36.2 1.1 broadcast_select_fusion.1
  37.3 1.2 pad_maximum_fusion.2.shard
  38.5 227.6 %shard_map.103 = (bf16[1024,16,128]{2,1,0:T(8,128)(2,1)}, bf16[1024,16,128]{2,1,0:T(8,128)(2,1)}, bf16[1024,16,128]{2,1,0:T(8,128)(2,1)}) custom-call(bf16[256,16,128]{2,1,0:T(8,128)(2,1)} %pad_maximum_fusion.2.shard, bf16[1024,1024]{1,0:T(8,128)(2,1)} %pad_maximum_fusion.1.weights, bf16[2048,512]{1,0:T(8,128)(2,1)} %bitcast.8, bf16[2048,512]{1,0:T(8,128)(2,1)} %bitcast.9, ...), custom_call_target="tpu_custom_call" | custom-call | flops 15000000512 | bytes 100000000 | tf_op jit(solution)/shard_map/pallas_call | solution.py:492
  266.1 0.0 copy-start.10
  266.2 0.0 copy-start.12
  266.2 5.0 %fusion.14.dual = bf16[16,128,512]{2,1,0:T(8,128)(2,1)S(1)} fusion(bf16[1024,512,1]{1,0,2:T(8,128)(2,1)S(1)} %fusion.20, bf16[1024,16,128]{2,1,0:T(8,128)(2,1)} %get-tuple-element.13), kind=kOutput, calls=%fused_computation.17 | convolution fusion | flops 2148532224 | bytes 7340032 | tf_op jit(solution)/shard_map/ka,kzr->zra/dot_general | solution.py:567
  271.1 0.0 copy-start.4
  271.2 2.0 collective-permute-start.6
  273.2 3.7 %collective-permute-start.5 = (bf16[1,128,512]{2,1,0:T(8,128)(2,1)S(1)}, bf16[1,128,512]{2,1,0:T(8,128)(2,1)S(1)}, u32[]{:S(2)}, u32[]{:S(2)}) collective-permute-start(bf16[1,128,512]{2,1,0:T(8,128)(2,1)S(1)} %get-tuple-element.19), channel_id=1, source_target_pairs={{0,2},{2,4},{4,6},{6,8},{8,10},{10,12},{12,14},{14,16},{16,18},{18... | collective-permute-start | bytes 393224 | tf_op jit(solution)/shard_map/ppermute | solution.py:22
  276.9 0.0 copy-done.10
  276.9 0.0 copy-done.12
  276.9 0.0 copy-start.11
  277.0 5.2 %fusion.7 = (bf16[16,512]{1,0:T(8,128)(2,1)}, bf16[16,128,512]{2,1,0:T(8,128)(2,1)}) fusion(s32[16,512]{1,0:T(8,128)S(1)} %copy-done.10, bf16[1024,512,1]{1,0,2:T(8,128)(2,1)S(1)} %fusion.20, bf16[1024,16,128]{2,1,0:T(8,128)(2,1)S(1)} %copy-done.12), kind=kOutput, calls=%fused_computation.8 | convolution fusion | flops 2151669760 | bytes 7389184 | tf_op jit(solution)/shard_map/ka,kzr->zra/dot_general | solution.py:567
  282.1 0.0 copy-done.4
  282.1 0.0 copy-done.11
  282.1 3.9 %fusion.11 = bf16[16,128,512]{2,1,0:T(8,128)(2,1)} fusion(bf16[1024,512,1]{1,0,2:T(8,128)(2,1)S(1)} %fusion.20, bf16[1024,16,128]{2,1,0:T(8,128)(2,1)S(1)} %copy-done.11), kind=kOutput, calls=%fused_computation.16 | convolution fusion | flops 2148532224 | bytes 7340032 | tf_op jit(solution)/shard_map/ka,kzr->zra/dot_general | solution.py:567
  286.1 0.0 collective-permute-done.6.dual_after
  286.1 0.0 copy-start.8
  286.1 0.0 collective-permute-done.5.dual_before
  286.1 0.6 copy-done.8
  286.7 0.0 copy-start.9
  286.7 0.7 copy-done.9
  287.4 7.7 %shard_map.104 = f32[16,128,512]{2,1,0:T(8,128)} custom-call(s32[16,512]{1,0:T(8,128)} %wet.3, f32[16,128,512]{2,1,0:T(8,128)} %heat.3, bf16[16,128,512]{2,1,0:T(8,128)(2,1)} %copy-done.4, bf16[1,128,512]{2,1,0:T(8,128)(2,1)} %copy-done.9, bf16[1,128,512]{2,1,0:T(8,128)(2,1)} %copy-done.8), custom_call_target="tpu_custom_call" | custom-call | flops 10485760 | bytes 6291456 | tf_op jit(solution)/shard_map/pallas_call | solution.py:75
  (1 shorter events, 0.0 us)
Async XLA Ops:
  0.6 17.8 %copy-start.5 = (bf16[1024,1024]{1,0:T(8,128)(2,1)S(1)}, bf16[1024,1024]{1,0:T(8,128)(2,1)}, u32[]{:S(2)}) copy-start(bf16[1024,1024]{1,0:T(8,128)(2,1)} %constant.27.clone) | copy-start | bytes 6291460
  2.7 23.9 %collective-permute-start.4 = (f32[1,128,512]{2,1,0:T(8,128)}, f32[1,128,512]{2,1,0:T(8,128)S(1)}, u32[]{:S(2)}, u32[]{:S(2)}) collective-permute-start(f32[1,128,512]{2,1,0:T(8,128)} %get-tuple-element.14), channel_id=1, source_target_pairs={{2,0},{4,2},{6,4},{8,6},{10,8},{12,10},{14,12},{16,14},{18,16},{20... | collective-permute-start | bytes 786440 | tf_op jit(solution)/shard_map/ppermute | solution.py:23
  4.6 21.9 %collective-permute-start.3 = (f32[1,128,512]{2,1,0:T(8,128)}, f32[1,128,512]{2,1,0:T(8,128)}, u32[]{:S(2)}, u32[]{:S(2)}) collective-permute-start(f32[1,128,512]{2,1,0:T(8,128)} %get-tuple-element.15), channel_id=1, source_target_pairs={{0,2},{2,4},{4,6},{6,8},{8,10},{10,12},{12,14},{14,16},{16,18},{18... | collective-permute-start | bytes 786440 | tf_op jit(solution)/shard_map/ppermute | solution.py:22
  11.0 15.6 %collective-permute-start.2 = (f32[1,128,512]{2,1,0:T(8,128)}, f32[1,128,512]{2,1,0:T(8,128)}, u32[]{:S(2)}, u32[]{:S(2)}) collective-permute-start(f32[1,128,512]{2,1,0:T(8,128)} %get-tuple-element.16), channel_id=1, source_target_pairs={{2,0},{4,2},{6,4},{8,6},{10,8},{12,10},{14,12},{16,14},{18,16},{20... | collective-permute-start | bytes 786440 | tf_op jit(solution)/shard_map/ppermute | solution.py:23
  12.9 13.7 %collective-permute-start.1 = (f32[1,128,512]{2,1,0:T(8,128)}, f32[1,128,512]{2,1,0:T(8,128)}, u32[]{:S(2)}, u32[]{:S(2)}) collective-permute-start(f32[1,128,512]{2,1,0:T(8,128)} %get-tuple-element.17), channel_id=1, source_target_pairs={{0,2},{2,4},{4,6},{6,8},{8,10},{10,12},{12,14},{14,16},{16,18},{18... | collective-permute-start | bytes 786440 | tf_op jit(solution)/shard_map/ppermute | solution.py:22
  18.4 17.7 %collective-permute-start = (bf16[256,8,128]{2,1,0:T(8,128)(2,1)}, bf16[256,8,128]{2,1,0:T(8,128)(2,1)}, u32[]{:S(2)}, u32[]{:S(2)}) collective-permute-start(bf16[256,8,128]{2,1,0:T(8,128)(2,1)} %constant_dynamic-slice_fusion.6), channel_id=1, source_target_pairs={{0,2},{2,0},{4,6},{6,4},{8,10},{10,8},{12,14},{14,12},{16,18},{18,... | collective-permute-start | bytes 1572872 | tf_op jit(solution)/shard_map/ppermute | solution.py:530
  18.7 0.8 copy-start
  18.7 1.0 copy-start.2
  23.7 1.0 copy-start.1
  23.7 1.2 copy-start.3
  26.5 9.6 %copy-start.6 = (bf16[512,8,128]{2,1,0:T(8,128)(2,1)S(1)}, bf16[512,8,128]{2,1,0:T(8,128)(2,1)}, u32[]{:S(2)}) copy-start(bf16[512,8,128]{2,1,0:T(8,128)(2,1)} %param.12) | copy-start | bytes 3145732
  26.6 0.7 copy-start.7
  266.1 10.8 %copy-start.10 = (s32[16,512]{1,0:T(8,128)S(1)}, s32[16,512]{1,0:T(8,128)}, u32[]{:S(2)}) copy-start(s32[16,512]{1,0:T(8,128)} %param.11) | copy-start | bytes 98308
  266.2 10.8 %copy-start.12 = (bf16[1024,16,128]{2,1,0:T(8,128)(2,1)S(1)}, bf16[1024,16,128]{2,1,0:T(8,128)(2,1)}, u32[]{:S(2)}) copy-start(bf16[1024,16,128]{2,1,0:T(8,128)(2,1)} %get-tuple-element.11) | copy-start | bytes 12582916
  271.1 11.0 %copy-start.4 = (bf16[16,128,512]{2,1,0:T(8,128)(2,1)}, bf16[16,128,512]{2,1,0:T(8,128)(2,1)S(1)}, u32[]{:S(2)}) copy-start(bf16[16,128,512]{2,1,0:T(8,128)(2,1)S(1)} %fusion.14.dual) | copy-start | bytes 6291460
  271.2 14.9 %collective-permute-start.6 = (bf16[1,128,512]{2,1,0:T(8,128)(2,1)S(1)}, bf16[1,128,512]{2,1,0:T(8,128)(2,1)S(1)}, u32[]{:S(2)}, u32[]{:S(2)}) collective-permute-start(bf16[1,128,512]{2,1,0:T(8,128)(2,1)S(1)} %get-tuple-element.18), channel_id=1, source_target_pairs={{2,0},{4,2},{6,4},{8,6},{10,8},{12,10},{14,12},{16,14},{18,16},{20... | collective-permute-start | bytes 393224 | tf_op jit(solution)/shard_map/ppermute | solution.py:23
  273.2 12.9 %collective-permute-start.5 = (bf16[1,128,512]{2,1,0:T(8,128)(2,1)S(1)}, bf16[1,128,512]{2,1,0:T(8,128)(2,1)S(1)}, u32[]{:S(2)}, u32[]{:S(2)}) collective-permute-start(bf16[1,128,512]{2,1,0:T(8,128)(2,1)S(1)} %get-tuple-element.19), channel_id=1, source_target_pairs={{0,2},{2,4},{4,6},{6,8},{8,10},{10,12},{12,14},{14,16},{16,18},{18... | collective-permute-start | bytes 393224 | tf_op jit(solution)/shard_map/ppermute | solution.py:22
  276.9 5.2 %copy-start.11 = (bf16[1024,16,128]{2,1,0:T(8,128)(2,1)S(1)}, bf16[1024,16,128]{2,1,0:T(8,128)(2,1)}, u32[]{:S(2)}) copy-start(bf16[1024,16,128]{2,1,0:T(8,128)(2,1)} %get-tuple-element.12) | copy-start | bytes 12582916
  286.1 0.6 copy-start.8
  286.7 0.7 copy-start.9
where the time goes:
time: 296 us; the launch traced here: 295 us
  Pallas kernels  244 us (82%)
  starting transfers between devices  17.7 us (6%)
  matrix products  14.1 us (5%)
  local copies, waits for them, and re-layouts  10.2 us (3%)
  other arithmetic  7.97 us (3%)
    pallas_call x1, Pallas kernels, solved_modes(): pl.pallas_call(modes_kernel, out_shape=[out] * fields, in_specs=[pl.Block...  228 us
    pallas_call x2, Pallas kernels, by_radius(): pl.pallas_call(kernel, grid=(radial // rows,), in_specs=[pl.BlockSpec(wet...  16.6 us
    dot_general x3, matrix products, inverse(): jnp.einsum('ka,kzr->zra', to_azimuths, solved, preferred_element_type=jnp...  14.1 us
    ppermute x3, starting transfers between devices, halo_planes(): before = lax.ppermute(last, 'depth', up)  11.8 us
  transfers between devices with their start and end apart: 7, of which 0 were waited for; matrix products, arithmetic and copies ran while one was open for 6% of the time, Pallas kernels for 3%

commit v1 on v0

--- a/solution.py
+++ b/solution.py
@@ -231,13 +231,13 @@
 
 
 def modes_kernel(
-    shard, weights, seed, forward, tangent,
+    shard, full, cotangent, heat, tangent, wet,
     out_seed, out_forward, out_tangent,
-    matrices, table, values, stage, mine, theirs, given,
+    matrices, table, values, stage, mine, theirs, given, raw, edges, damp,
     pair_send, pair_recv, up_send, up_recv, down_send, down_recv, azi_send, azi_recv,
-    twin_send, twin_recv, back_send, back_recv, keep_sem, load_sem,
+    twin_send, twin_recv, back_send, back_recv, keep_sem, load_sem, table_sem, raw_sem, edge_send, edge_recv,
 ):
-    sources, outs = (seed, forward, tangent), (out_seed, out_forward, out_tangent)
+    outs = (out_seed, out_forward, out_tangent)
     flips = (True, False, False)
     place, azi = lax.axis_index("depth"), lax.axis_index("azi")
     z, x, core = place // 4, place // 2 % 2, place % 2
@@ -247,7 +247,10 @@
     half = count // 2
     rows = shard.shape[1]
     slab = mine.shape[2]
-    local = seed.shape[1]
+    local = heat.shape[2]
+    strip = raw.shape[3]
+    strips = radial // strip
+    last = lax.axis_size("depth") - 1
     planes = slab // blocks
     mesh_ids = pl.DeviceIdType.MESH
 
@@ -268,7 +271,16 @@
     def _():
         greet(down, azi)
 
-    pl.semaphore_wait(barrier, 4 + (z + 1) // 2 % 2)
+    @pl.when(place < last)
+    def _():
+        greet(place + 1, azi)
+
+    @pl.when(place > 0)
+    def _():
+        greet(place - 1, azi)
+
+    inner = (place + last) // (last + 1) + (2 * last - place) // (last + 1)
+    pl.semaphore_wait(barrier, 4 + (z + 1) // 2 % 2 + inner)
 
     def remote(src, dst, send, recv, where, azimuth=azi):
         return pltpu.make_async_remote_copy(
@@ -364,16 +376,127 @@
                 down_copy(q, c, p).wait_send()
 
     at = pl.multiple_of(rows * (2 * z + x), rows)
-    loads = [pltpu.make_async_copy(shard, matrices.at[pl.ds(0, half), pl.ds(at, rows), :], load_sem.at[0])]
-    for f in range(fields):
-        loads.append(
-            pltpu.make_async_copy(sources[f], values.at[f, :, pl.ds(0, local)], load_sem.at[1 + f])
-        )
-    loads.append(pltpu.make_async_copy(weights, table, load_sem.at[1 + fields]))
-    for load in loads:
+    shard_load = pltpu.make_async_copy(
+        shard, matrices.at[pl.ds(0, half), pl.ds(at, rows), :], load_sem.at[0]
+    )
+    shard_load.start()
+    damp_load = pltpu.make_async_copy(wet, damp, load_sem.at[1])
+    damp_load.start()
+
+    def strip_loads(n):
+        slot = n % 2
+        c = n % strips
+        span = pl.ds(c * strip, strip)
+        if n < strips:
+            return [
+                pltpu.make_async_copy(
+                    cotangent.at[:, span, :], raw.at[slot, 0, pl.ds(1, slab)], raw_sem.at[slot, 0]
+                )
+            ]
+        found = []
+        for f, source in enumerate((heat, tangent)):
+            found.append((source.at[:, span, :], raw.at[slot, f, pl.ds(1, slab)], 3 * f))
+            found.append((edges.at[f, 0, span], raw.at[slot, f, 0], 3 * f + 1))
+            found.append((edges.at[f, 1, span], raw.at[slot, f, slab + 1], 3 * f + 2))
+        return [pltpu.make_async_copy(a, b, raw_sem.at[slot, i]) for a, b, i in found]
+
+    for load in strip_loads(0):
         load.start()
-    for load in loads:
-        load.wait()
+
+    def edge_copies(side):
+        out = []
+        for f, source in enumerate((heat, tangent)):
+            out.append(
+                remote(
+                    source.at[slab - 1 if side == 0 else 0], edges.at[f, side],
+                    edge_send.at[f, side], edge_recv.at[f, side],
+                    place + 1 if side == 0 else place - 1,
+                )
+            )
+        return out
+
+    def edges_out():
+        @pl.when(place < last)
+        def _():
+            for copy in edge_copies(0):
+                copy.start()
+
+        @pl.when(place > 0)
+        def _():
+            for copy in edge_copies(1):
+                copy.start()
+
+    def edges_in():
+        for side, empty, full_side in ((0, place == 0, place > 0), (1, place == last, place < last)):
+
+            @pl.when(full_side)
+            def _():
+                for copy in edge_copies(side):
+                    copy.wait_recv()
+
+            @pl.when(empty)
+            def _():
+                edges[:, side] = jnp.zeros((2, radial, local), jnp.float32)
+
+    def edges_sent():
+        @pl.when(place < last)
+        def _():
+            for copy in edge_copies(0):
+                copy.wait_send()
+
+        @pl.when(place > 0)
+        def _():
+            for copy in edge_copies(1):
+                copy.wait_send()
+
+    table_loads = []
+    for part in range(4):
+        owner, which = (azi, 1 - azi)[part % 2], (1 - core, core)[part // 2]
+        row = pl.multiple_of((2 * owner + which) * (half), half)
+        for h in range(2):
+            col = pl.multiple_of((azi, 1 - azi)[h] * local, local)
+            table_loads.append(
+                pltpu.make_async_copy(
+                    full.at[pl.ds(row, half), pl.ds(col, local)],
+                    table.at[pl.ds(part * half, half), pl.ds(h * local, local)],
+                    table_sem.at[part, h],
+                )
+            )
+
+    def prepare(n):
+        slot = n % 2
+        c = n % strips
+        if n + 1 == strips:
+            edges_in()
+        if n + 1 < 2 * strips:
+            for load in strip_loads(n + 1):
+                load.start()
+        for load in strip_loads(n):
+            load.wait()
+        radius = c * strip + lax.broadcasted_iota(jnp.int32, (strip, local), 0)
+        profile = evaporation * jnp.exp(-radius.astype(jnp.float32) / skin_depth)
+
+        def plane_step(p, _):
+            into = pl.ds(pl.multiple_of(p * radial + c * strip, strip), strip)
+            if n < strips:
+                values[0, into, pl.ds(0, local)] = raw[slot, 0, p + 1].astype(jnp.bfloat16)
+                return 0
+            damping = damp[pl.ds(p, 1), :].astype(jnp.float32) * profile
+
+            def mix(f):
+                centre = raw[slot, f, p + 1]
+                around = raw[slot, f, p + 2] + raw[slot, f, p]
+                return centre, centre + mixing * (around - 2.0 * centre)
+
+            centre, value = mix(0)
+            moisture = jnp.tanh(centre)
+            values[1, into, pl.ds(0, local)] = (value - damping * moisture).astype(jnp.bfloat16)
+            slope = 1.0 - moisture * moisture
+            centre, value = mix(1)
+            values[2, into, pl.ds(0, local)] = (value - damping * slope * centre).astype(jnp.bfloat16)
+            return 0
+
+        lax.fori_loop(0, slab, plane_step, 0)
 
     def twin_copy(f, part):
         at = pl.ds(part * half, half)
@@ -381,30 +504,39 @@
             given.at[f, at], theirs.at[f, at], twin_send.at[f, part], twin_recv.at[f, part], twin
         )
 
-    def transform(f, part):
-        into, first = (given, part) if part < 2 else (mine, part - 2)
-
+    group = 4
+
+    def transform(f, into, first):
         def planes_step(n, _):
-            cols = values[f, pl.ds(pl.multiple_of(n * 2 * radial, 2 * radial), 2 * radial), :]
+            span = group * radial
+            cols = values[f, pl.ds(pl.multiple_of(n * span, span), span), :]
             out = lax.dot_general(
-                table[pl.ds(part * half, half), :], cols, (((1,), (1,)), ((), ())),
+                table[pl.ds(first, count), :], cols, (((1,), (1,)), ((), ())),
                 preferred_element_type=jnp.float32,
             )
-            stage[pl.ds(pl.multiple_of(n * 2 * half, half), half), :] = out[:, :radial]
-            stage[pl.ds(pl.multiple_of(n * 2 * half + half, half), half), :] = out[:, radial:]
+            for g in range(group):
+                at = pl.multiple_of((n * group + g) * count, count)
+                stage[pl.ds(at, count), :] = out[:, g * radial : (g + 1) * radial]
             return 0
 
-        lax.fori_loop(0, slab // 2, planes_step, 0)
+        lax.fori_loop(0, slab // group, planes_step, 0)
 
         def turn(n, _):
             for u in range(8):
                 k = n * 8 + u
-                into[f, first * half + k] = stage[pl.ds(k, slab, stride=half), :].astype(jnp.bfloat16)
+                into[f, k] = stage[pl.ds(k, slab, stride=count), :].astype(jnp.bfloat16)
             return 0
 
-        lax.fori_loop(0, half // 8, turn, 0)
-        if part < 2:
-            twin_copy(f, part).start()
+        for part in range(2):
+            lax.fori_loop(part * half // 8, (part + 1) * half // 8, turn, 0)
+            if first == 0:
+                twin_copy(f, part).start()
+
+    def give(f):
+        transform(f, given, 0)
+
+    def take(f):
+        transform(f, mine, count)
 
     def keep_copy(f, q):
         at = pl.ds(q * step, step)
@@ -419,8 +551,9 @@
 
     def solve(which, q):
         def one(n, _):
-            for u in range(4):
-                k = q * step + n * 4 + u
+            found = []
+            for u in range(16):
+                k = q * step + n * 16 + u
                 matrix = matrices[k]
                 for flip in (True, False):
                     chosen = [f for f in which if flips[f] == flip]
@@ -432,13 +565,16 @@
                     out = lax.dot_general(
                         stacked, matrix, (((1,), (0 if flip else 1,)), ((), ())),
                         preferred_element_type=jnp.float32,
-                    ).astype(jnp.bfloat16)
-                    for i, f in enumerate(chosen):
-                        mine[f, k] = out[2 * i * slab : (2 * i + 1) * slab]
-                        theirs[f, k] = out[(2 * i + 1) * slab : (2 * i + 2) * slab]
+                    )
+                    found.append((chosen, k, out))
+            for chosen, k, out in found:
+                out = out.astype(jnp.bfloat16)
+                for i, f in enumerate(chosen):
+                    mine[f, k] = out[2 * i * slab : (2 * i + 1) * slab]
+                    theirs[f, k] = out[(2 * i + 1) * slab : (2 * i + 2) * slab]
             return 0
 
-        lax.fori_loop(0, step // 4, one, 0)
+        lax.fori_loop(0, step // 16, one, 0)
         for f in which:
             keep_copy(f, q).start()
             back_copy(f, q).start()
@@ -447,32 +583,49 @@
         for part in range(2):
             twin_copy(f, part).wait_recv()
 
-    tasks = {
-        13: [lambda: transform(0, 0), lambda: transform(0, 1)],
-        14: [lambda: transform(0, 2), lambda: transform(0, 3)],
-        16: [lambda: met(0), lambda: solve([0], 0)],
-        17: [lambda: solve([0], 1), lambda: solve([0], 2)],
-        18: [lambda: solve([0], 3)],
-        21: [lambda: transform(1, 0), lambda: transform(1, 1)],
-        22: [lambda: transform(1, 2), lambda: transform(1, 3)],
-        24: [lambda: met(1), lambda: solve([1], 0), lambda: solve([1], 1)],
-        25: [lambda: solve([1], 2)],
-        26: [lambda: solve([1], 3)],
-        29: [functools.partial(transform, 2, part) for part in range(4)]
-        + [lambda: solve([0, 1], 4)],
-        30: [lambda: solve([0, 1], 7), lambda: solve([0, 1], 5), lambda: met(2)]
-        + [functools.partial(solve, [2], q) for q in (0, 1, 2, 3, 4, 7, 5)],
-        31: [lambda: solve([0, 1, 2], 6)],
+    def begin():
+        edges_out()
+        for load in table_loads:
+            load.start()
+        damp_load.wait()
+        for n in range(4):
+            prepare(n)
+
+    def table_in():
+        for load in table_loads:
+            load.wait()
+
+    P = functools.partial
+    tasks = {0: [begin], 1: [P(prepare, n) for n in range(4, strips)], 2: [table_in]}
+    for n in range(strips):
+        tasks.setdefault(2 + n, []).append(P(prepare, strips + n))
+    tasks |= {
+        13: [P(give, 0)],
+        14: [P(take, 0)],
+        16: [P(met, 0), P(solve, [0], 0), P(solve, [0], 1)],
+        17: [P(solve, [0], 2)],
+        18: [P(solve, [0], 3)],
+        21: [P(give, 1)],
+        22: [P(take, 1)],
+        24: [P(met, 1), P(solve, [1], 0), P(solve, [1], 1)],
+        25: [P(solve, [1], 2), P(solve, [1], 3)],
+        28: [P(solve, [0], 4), P(solve, [0], 7)],
+        29: [P(give, 2), P(take, 2), P(solve, [0], 5)],
+        30: [P(solve, [0], 6), P(met, 2)]
+        + [P(solve, [2], q) for q in range(early)]
+        + [P(solve, [1, 2], q) for q in (4, 7, 5, 6)],
     }
 
+    shard_load.wait()
     lag = 2
-    for t in range(32):
+    for t in range(31):
         receive(t - lag)
         send(t)
         for task in tasks.get(t, []):
             task()
 
-    for t in range(32):
+    edges_sent()
+    for t in range(31):
         sent(t)
     for f in range(fields):
         for part in range(2):
@@ -482,39 +635,43 @@
             back_copy(f, q).wait()
 
 
-def solved_modes(shard, weights, seed, forward, tangent):
-    slab, radial, local = seed.shape
+def solved_modes(shard, table, cotangent, heat, tangent, wet):
+    slab, radial, local = heat.shape
     half, rows, _ = shard.shape
     count = 2 * half
+    strip = 16
     dma = pltpu.SemaphoreType.DMA
-    flat = [v.reshape(slab * radial, local) for v in (seed, forward, tangent)]
     out = jax.ShapeDtypeStruct((2 * count, slab, radial), jnp.bfloat16)
+    modes = pltpu.VMEM((fields, count, slab, radial), jnp.bfloat16)
     return pl.pallas_call(
         modes_kernel,
         out_shape=[out] * fields,
-        in_specs=[pl.BlockSpec(memory_space=pl.ANY)] * 5,
+        in_specs=[pl.BlockSpec(memory_space=pl.ANY)] * 6,
         out_specs=[pl.BlockSpec(memory_space=pl.ANY)] * fields,
         scratch_shapes=[
             pltpu.VMEM((count, radial, radial), jnp.bfloat16),
             pltpu.VMEM((2 * count, 2 * local), jnp.bfloat16),
             pltpu.VMEM((fields, slab * radial, 2 * local), jnp.bfloat16),
-            pltpu.VMEM((slab * half, radial), jnp.float32),
-            pltpu.VMEM((fields, count, slab, radial), jnp.bfloat16),
-            pltpu.VMEM((fields, count, slab, radial), jnp.bfloat16),
-            pltpu.VMEM((fields, count, slab, radial), jnp.bfloat16),
+            pltpu.VMEM((slab * count, radial), jnp.float32),
+            modes,
+            modes,
+            modes,
+            pltpu.VMEM((2, 2, slab + 2, strip, local), jnp.float32),
+            pltpu.VMEM((2, 2, radial, local), jnp.float32),
+            pltpu.VMEM((slab, local), jnp.int32),
             dma((blocks, 4)), dma((blocks, 4)),
             dma((blocks + 1, 3)), dma((blocks + 1, 3)),
             dma((blocks + 1, 3)), dma((blocks + 1, 3)),
             dma((early + fields * blocks,)), dma((early + fields * blocks,)),
             dma((fields, 2)), dma((fields, 2)),
             dma((fields, blocks)), dma((fields, blocks)), dma((fields, blocks)),
-            dma((fields + 2,)),
+            dma((2,)), dma((4, 2)), dma((2, 6)), dma((2, 2)), dma((2, 2)),
         ],
         compiler_params=pltpu.CompilerParams(
-            collective_id=0, has_side_effects=True, vmem_limit_bytes=58 * 1024 * 1024
+            collective_id=0, has_side_effects=True, vmem_limit_bytes=60 * 1024 * 1024
         ),
         cost_estimate=pl.CostEstimate(flops=15 * 10**9, bytes_accessed=10**8, transcendentals=0),
-    )(shard, weights, *flat)
+    )(shard, table, cotangent, heat, tangent, wet)
 
 
 def fused_body(table, heat_state, tangent_in, cotangent, wet_mask, sensors, propagators):
@@ -544,23 +701,10 @@
     def columns(weights, owner):
         return lax.dynamic_slice_in_dim(weights, owner * local_azi, local_azi, axis=1)
 
-    weights = jnp.concatenate([twin_rows, own_rows], axis=0)
-    weights = jnp.concatenate([columns(weights, me), columns(weights, 1 - me)], axis=1)
     to_azimuths = columns(jnp.concatenate([own_rows, twin_rows], axis=0), me)
 
-    forward_rhs, tangent_rhs = by_radius(
-        rhs_kernel,
-        wet_mask,
-        [
-            heat_state,
-            *halo_planes(heat_state[-1:], heat_state[:1]),
-            tangent_in,
-            *halo_planes(tangent_in[-1:], tangent_in[:1]),
-        ],
-        [jnp.bfloat16] * 2,
-    )
     dual_modes, forward_modes, tangent_modes = solved_modes(
-        shard, weights, cotangent.astype(jnp.bfloat16), forward_rhs, tangent_rhs
+        shard, table, cotangent, heat_state, tangent_in, wet_mask
     )
 
     def inverse(solved):

time: 296 us -> 245 us (0.83)
  Pallas kernels: 244 us -> 216 us
  starting transfers between devices: 17.7 us -> 5.86 us
  other arithmetic: 7.97 us -> 1.34 us
  local copies, waits for them, and re-layouts: 10.2 us -> 5.23 us
    pallas_call x1, Pallas kernels: 228 us -> 208 us  [solved_modes(): pl.pallas_call(modes_kernel, out_shape=[out] * fields, in_specs=[pl.Block...]
    pallas_call x2 -> x1, Pallas kernels: 16.6 us -> 7.71 us  [by_radius(): pl.pallas_call(kernel, grid=(radial // rows,), in_specs=[pl.BlockSpec(wet...]
    ppermute x3 -> x1, starting transfers between devices: 11.8 us -> 3.28 us  [halo_planes(): before = lax.ppermute(last, 'depth', up)]
    slice x2 -> x0, local copies, waits for them, and re-layouts: 3.91 us -> none  [the longest x1 2.04 us: fused_body(): tangent_in[:1]]
    convert_element_type x1 -> x0, other arithmetic: 3.8 us -> none  [fused_body(): cotangent.astype(jnp.bfloat16)]
    ppermute x3 -> x1, starting transfers between devices: 5.91 us -> 2.46 us  [halo_planes(): after = lax.ppermute(first, 'depth', down)]
  transfers between devices with their start and end apart: 7 -> 3, of which waited for: 0 -> 0; matrix products, arithmetic and copies ran while one was open for 6% -> 5% of each run, Pallas kernels for 3% -> 0%
where the time goes in v1:
time: 245 us; the launch traced here: 243 us
  Pallas kernels  216 us (88%)
  matrix products  14.1 us (6%)
  starting transfers between devices  5.86 us (2%)
  local copies, waits for them, and re-layouts  5.23 us (2%)
    pallas_call x1, Pallas kernels, solved_modes(): pl.pallas_call(modes_kernel, out_shape=[out] * fields, in_specs=[pl.Block...  208 us
    dot_general x3, matrix products, inverse(): jnp.einsum('ka,kzr->zra', to_azimuths, solved, preferred_element_type=jnp...  14.1 us
    pallas_call x1, Pallas kernels, by_radius(): pl.pallas_call(kernel, grid=(radial // rows,), in_specs=[pl.BlockSpec(wet...  7.71 us
  transfers between devices with their start and end apart: 3, of which 0 were waited for; matrix products, arithmetic and copies ran while one was open for 5% of the time, Pallas kernels for 0%

profile of v1, /device:TPU:1, one launch (start us, length us, event | category | flops | bytes accessed | tf_op | source)
XLA Modules:
  0.0 242.8 jit_solution(13313299152245909243)
XLA Ops:
  0.6 1.1 constant_dynamic-slice_fusion.4
  1.7 0.1 collective-permute-start
  1.8 1.7 constant_dynamic-slice_fusion
  3.6 0.0 copy-start.1
  3.6 0.1 fusion.20
  3.7 0.0 collective-permute-done
  3.7 1.1 copy-done.1
  4.8 0.1 broadcast_select_fusion.1
  4.9 1.2 pad_maximum_fusion.shard
  6.0 207.8 %shard_map.102 = (bf16[1024,16,128]{2,1,0:T(8,128)(2,1)}, bf16[1024,16,128]{2,1,0:T(8,128)(2,1)}, bf16[1024,16,128]{2,1,0:T(8,128)(2,1)}) custom-call(bf16[256,16,128]{2,1,0:T(8,128)(2,1)} %pad_maximum_fusion.shard, bf16[1024,1024]{1,0:T(8,128)(2,1)} %constant.27.clone.full, f32[16,128,512]{2,1,0:T(8,128)} %cotangent.1, f32[16,128,512]{2,1,0:T(8,128)} %heat.3, ...), custom_call_target="tpu_custom_call" | custom-call | flops 15000000512 | bytes 100000000 | tf_op jit(solution)/shard_map/pallas_call | solution.py:646
  213.9 0.0 copy-start.4
  213.9 0.0 copy-start.6
  213.9 5.0 %fusion.14.dual = bf16[16,128,512]{2,1,0:T(8,128)(2,1)S(1)} fusion(bf16[1024,512,1]{1,0,2:T(8,128)(2,1)S(1)} %fusion.20, bf16[1024,16,128]{2,1,0:T(8,128)(2,1)} %get-tuple-element.9), kind=kOutput, calls=%fused_computation.15 | convolution fusion | flops 2148532224 | bytes 7340032 | tf_op jit(solution)/shard_map/ka,kzr->zra/dot_general | solution.py:711
  218.9 0.0 copy-start
  218.9 2.5 %collective-permute-start.2 = (bf16[1,128,512]{2,1,0:T(8,128)(2,1)S(1)}, bf16[1,128,512]{2,1,0:T(8,128)(2,1)S(1)}, u32[]{:S(2)}, u32[]{:S(2)}) collective-permute-start(bf16[1,128,512]{2,1,0:T(8,128)(2,1)S(1)} %get-tuple-element.10), channel_id=1, source_target_pairs={{2,0},{4,2},{6,4},{8,6},{10,8},{12,10},{14,12},{16,14},{18,16},{20... | collective-permute-start | bytes 393224 | tf_op jit(solution)/shard_map/ppermute | solution.py:23
  221.4 3.3 %collective-permute-start.1 = (bf16[1,128,512]{2,1,0:T(8,128)(2,1)S(1)}, bf16[1,128,512]{2,1,0:T(8,128)(2,1)S(1)}, u32[]{:S(2)}, u32[]{:S(2)}) collective-permute-start(bf16[1,128,512]{2,1,0:T(8,128)(2,1)S(1)} %get-tuple-element.11), channel_id=1, source_target_pairs={{0,2},{2,4},{4,6},{6,8},{8,10},{10,12},{12,14},{14,16},{16,18},{18... | collective-permute-start | bytes 393224 | tf_op jit(solution)/shard_map/ppermute | solution.py:22
  224.6 0.0 copy-done.4
  224.7 0.0 copy-done.6
  224.7 0.0 copy-start.5
  224.7 5.2 %fusion.7 = (bf16[16,512]{1,0:T(8,128)(2,1)}, bf16[16,128,512]{2,1,0:T(8,128)(2,1)}) fusion(s32[16,512]{1,0:T(8,128)S(1)} %copy-done.4, bf16[1024,512,1]{1,0,2:T(8,128)(2,1)S(1)} %fusion.20, bf16[1024,16,128]{2,1,0:T(8,128)(2,1)S(1)} %copy-done.6), kind=kOutput, calls=%fused_computation.8 | convolution fusion | flops 2151669760 | bytes 7389184 | tf_op jit(solution)/shard_map/ka,kzr->zra/dot_general | solution.py:711
  229.9 0.0 copy-done
  229.9 0.0 copy-done.5
  229.9 3.9 %fusion.11 = bf16[16,128,512]{2,1,0:T(8,128)(2,1)} fusion(bf16[1024,512,1]{1,0,2:T(8,128)(2,1)S(1)} %fusion.20, bf16[1024,16,128]{2,1,0:T(8,128)(2,1)S(1)} %copy-done.5), kind=kOutput, calls=%fused_computation.14 | convolution fusion | flops 2148532224 | bytes 7340032 | tf_op jit(solution)/shard_map/ka,kzr->zra/dot_general | solution.py:711
  233.8 0.0 collective-permute-done.2.dual_after
  233.8 0.0 copy-start.2
  233.8 0.0 collective-permute-done.1.dual_before
  233.8 0.6 copy-done.2
  234.4 0.0 copy-start.3
  234.5 0.6 copy-done.3
  235.1 7.7 %shard_map.103 = f32[16,128,512]{2,1,0:T(8,128)} custom-call(s32[16,512]{1,0:T(8,128)} %wet.3, f32[16,128,512]{2,1,0:T(8,128)} %heat.3, bf16[16,128,512]{2,1,0:T(8,128)(2,1)} %copy-done, bf16[1,128,512]{2,1,0:T(8,128)(2,1)} %copy-done.3, bf16[1,128,512]{2,1,0:T(8,128)(2,1)} %copy-done.2), custom_call_target="tpu_custom_call" | custom-call | flops 10485760 | bytes 6291456 | tf_op jit(solution)/shard_map/pallas_call | solution.py:75
  (1 shorter events, 0.0 us)
Async XLA Ops:
  1.7 2.0 collective-permute-start
  3.6 1.2 copy-start.1
  213.9 10.8 %copy-start.4 = (s32[16,512]{1,0:T(8,128)S(1)}, s32[16,512]{1,0:T(8,128)}, u32[]{:S(2)}) copy-start(s32[16,512]{1,0:T(8,128)} %param.11) | copy-start | bytes 98308
  213.9 10.8 %copy-start.6 = (bf16[1024,16,128]{2,1,0:T(8,128)(2,1)S(1)}, bf16[1024,16,128]{2,1,0:T(8,128)(2,1)}, u32[]{:S(2)}) copy-start(bf16[1024,16,128]{2,1,0:T(8,128)(2,1)} %get-tuple-element.7) | copy-start | bytes 12582916
  218.9 11.0 %copy-start = (bf16[16,128,512]{2,1,0:T(8,128)(2,1)}, bf16[16,128,512]{2,1,0:T(8,128)(2,1)S(1)}, u32[]{:S(2)}) copy-start(bf16[16,128,512]{2,1,0:T(8,128)(2,1)S(1)} %fusion.14.dual) | copy-start | bytes 6291460
  218.9 14.9 %collective-permute-start.2 = (bf16[1,128,512]{2,1,0:T(8,128)(2,1)S(1)}, bf16[1,128,512]{2,1,0:T(8,128)(2,1)S(1)}, u32[]{:S(2)}, u32[]{:S(2)}) collective-permute-start(bf16[1,128,512]{2,1,0:T(8,128)(2,1)S(1)} %get-tuple-element.10), channel_id=1, source_target_pairs={{2,0},{4,2},{6,4},{8,6},{10,8},{12,10},{14,12},{16,14},{18,16},{20... | collective-permute-start | bytes 393224 | tf_op jit(solution)/shard_map/ppermute | solution.py:23
  221.4 12.4 %collective-permute-start.1 = (bf16[1,128,512]{2,1,0:T(8,128)(2,1)S(1)}, bf16[1,128,512]{2,1,0:T(8,128)(2,1)S(1)}, u32[]{:S(2)}, u32[]{:S(2)}) collective-permute-start(bf16[1,128,512]{2,1,0:T(8,128)(2,1)S(1)} %get-tuple-element.11), channel_id=1, source_target_pairs={{0,2},{2,4},{4,6},{6,8},{8,10},{10,12},{12,14},{14,16},{16,18},{18... | collective-permute-start | bytes 393224 | tf_op jit(solution)/shard_map/ppermute | solution.py:22
  224.7 5.2 %copy-start.5 = (bf16[1024,16,128]{2,1,0:T(8,128)(2,1)S(1)}, bf16[1024,16,128]{2,1,0:T(8,128)(2,1)}, u32[]{:S(2)}) copy-start(bf16[1024,16,128]{2,1,0:T(8,128)(2,1)} %get-tuple-element.8) | copy-start | bytes 12582916
  233.8 0.6 copy-start.2
  234.4 0.6 copy-start.3

commit v2 on v1

--- a/solution.py
+++ b/solution.py
@@ -213,21 +213,39 @@
 
 
 fields = 3
-blocks = 8
-early = blocks // 2
+parts = 8
+early = parts // 2
+bounds = (0, 2, 4, 6, 8, 10, 12, 13, 15, 16)
+blocks = len(bounds) - 1
+sections = ((0, 1, 2), (3, 4, 5), (6, 7, 8))
+crossed = (7, 8)
 own, other = 0, 1
+ticks = 32
+
+
+def timed(items):
+    found = [[] for _ in range(ticks)]
+    start = 0
+    for item in items:
+        found[start // 2].append(item)
+        start += bounds[item[0] + 1] - bounds[item[0]]
+    return found
 
 
 def line_order():
-    first = [(q, own, p) for p in range(3) for q in range(early)]
-    later = [(q, own) for q in range(early, blocks)] + [(blocks - 1, other)]
-    return first + [(q, c, p) for p in range(3) for q, c in later]
+    found = []
+    for section in sections:
+        group = [(q, c) for q in section for c in ((own, other) if q in crossed else (own,))]
+        found += [(q, c, p) for p in range(3) for q, c in group]
+    return timed(found)
 
 
 def pair_order():
-    first = [(q, s) for s in range(4) for q in range(early)]
-    first.insert(10, (blocks - 1, 0))
-    return first + [(q, s) for s in range(4) for q in range(early, blocks - 1)]
+    found = []
+    for section in sections:
+        found += [(q, s) for s in range(4) for q in section if q not in crossed]
+    found[10:10] = [(q, 0) for q in crossed]
+    return timed(found)
 
 
 def modes_kernel(
@@ -242,16 +260,17 @@
     place, azi = lax.axis_index("depth"), lax.axis_index("azi")
     z, x, core = place // 4, place // 2 % 2, place % 2
     pair, twin, up, down = place + 2 - 4 * x, place + 1 - 2 * core, place + 4, place - 4
-    count, radial, _ = matrices.shape
-    step = count // blocks
+    count, radial = matrices.shape[1], matrices.shape[3]
+    step = count // parts
+    fine = count // bounds[-1]
     half = count // 2
-    rows = shard.shape[1]
+    chips = matrices.shape[0]
     slab = mine.shape[2]
     local = heat.shape[2]
     strip = raw.shape[3]
     strips = radial // strip
     last = lax.axis_size("depth") - 1
-    planes = slab // blocks
+    planes = slab // parts
     mesh_ids = pl.DeviceIdType.MESH
 
     barrier = pltpu.get_barrier_semaphore()
@@ -288,9 +307,11 @@
             device_id=(where, azimuth), device_id_type=mesh_ids,
         )
 
+    def span_of(q):
+        return pl.ds(bounds[q] * fine, (bounds[q + 1] - bounds[q]) * fine)
+
     def region(q, line, side):
-        at = pl.multiple_of(rows * (2 * line + side), rows)
-        return matrices.at[pl.ds(q * step, step), pl.ds(at, rows), :]
+        return matrices.at[2 * line + side, span_of(q)]
 
     flipped = (z, z + 1 - 2 * (z % 2), z + 2 - 4 * (z // 2), 3 - z)
 
@@ -299,7 +320,7 @@
         return remote(ref, ref, pair_send.at[q, s], pair_recv.at[q, s], pair)
 
     def line_item(q, c):
-        return blocks if c == other else q
+        return blocks + crossed.index(q) if c == other else q
 
     def up_copy(q, c, p):
         ref = region(q, z - p, x if c == own else 1 - x)
@@ -313,10 +334,10 @@
 
     def azi_copy(n):
         if n < early:
-            return remote(
-                region(n, z, x), region(n + early, z, x), azi_send.at[n], azi_recv.at[n], place, 1 - azi
-            )
-        f, part = divmod(n - early, blocks)
+            mine_at = matrices.at[2 * z + x, pl.ds(n * step, step)]
+            theirs_at = matrices.at[2 * z + x, pl.ds(half + n * step, step)]
+            return remote(mine_at, theirs_at, azi_send.at[n], azi_recv.at[n], place, 1 - azi)
+        f, part = divmod(n - early, parts)
         span = planes * radial
         at = pl.ds(part * span, span)
         return remote(
@@ -325,15 +346,23 @@
             azi_send.at[n], azi_recv.at[n], place, 1 - azi,
         )
 
-    pairs, lines, azis = pair_order(), line_order(), early + fields * blocks
+    pairs, lines, azis = pair_order(), line_order(), early + fields * parts
+
+    lag, lead = 2, 2
+
+    def each(t, act):
+        if 0 <= t < ticks:
+            for item in pairs[t]:
+                act(pair_copy(*item))
+
+    def azi_send_up_to(t):
+        for n in range(0 if t == 0 else t + lead, min(t + lead + 1, azis)):
+            azi_copy(n).start()
 
     def send(t):
-        if t < len(pairs):
-            pair_copy(*pairs[t]).start()
-        if t < azis:
-            azi_copy(t).start()
-        if t < len(lines):
-            q, c, p = lines[t]
+        each(t, lambda copy: copy.start())
+        azi_send_up_to(t)
+        for q, c, p in lines[t] if t < ticks else ():
 
             @pl.when((z < 3) & (z >= p))
             def _():
@@ -344,12 +373,11 @@
                 down_copy(q, c, p).start()
 
     def receive(t):
-        if 0 <= t < len(pairs):
-            pair_copy(*pairs[t]).wait_recv()
-        if 0 <= t < azis:
-            azi_copy(t).wait_recv()
-        if 0 <= t < len(lines):
-            q, c, p = lines[t]
+        if t >= 0:
+            for n in range(0 if t == 0 else t + lead, min(t + lead + 1, azis)):
+                azi_copy(n).wait_recv()
+        each(t, lambda copy: copy.wait_recv())
+        for q, c, p in lines[t] if 0 <= t < ticks else ():
 
             @pl.when(z >= p + 1)
             def _():
@@ -360,12 +388,10 @@
                 down_copy(q, c, p).wait_recv()
 
     def sent(t):
-        if t < len(pairs):
-            pair_copy(*pairs[t]).wait_send()
+        each(t, lambda copy: copy.wait_send())
         if t < azis:
             azi_copy(t).wait_send()
-        if t < len(lines):
-            q, c, p = lines[t]
+        for q, c, p in lines[t]:
 
             @pl.when((z < 3) & (z >= p))
             def _():
@@ -375,9 +401,8 @@
             def _():
                 down_copy(q, c, p).wait_send()
 
-    at = pl.multiple_of(rows * (2 * z + x), rows)
     shard_load = pltpu.make_async_copy(
-        shard, matrices.at[pl.ds(0, half), pl.ds(at, rows), :], load_sem.at[0]
+        shard, matrices.at[2 * z + x, pl.ds(0, half)], load_sem.at[0]
     )
     shard_load.start()
     damp_load = pltpu.make_async_copy(wet, damp, load_sem.at[1])
@@ -501,51 +526,54 @@
     def twin_copy(f, part):
         at = pl.ds(part * half, half)
         return remote(
-            given.at[f, at], theirs.at[f, at], twin_send.at[f, part], twin_recv.at[f, part], twin
+            given.at[f % 2, at], theirs.at[f, at], twin_send.at[f, part], twin_recv.at[f, part], twin
         )
 
     group = 4
 
-    def transform(f, into, first):
-        def planes_step(n, _):
-            span = group * radial
-            cols = values[f, pl.ds(pl.multiple_of(n * span, span), span), :]
+    def transform(f, n):
+        span = group * radial
+        cols = values[f, pl.ds(n * span, span), :]
+
+        def half_step(h, _):
+            weights = table[pl.ds(pl.multiple_of(h * count, count), count), :]
             out = lax.dot_general(
-                table[pl.ds(first, count), :], cols, (((1,), (1,)), ((), ())),
-                preferred_element_type=jnp.float32,
+                weights, cols, (((1,), (1,)), ((), ())), preferred_element_type=jnp.float32
             )
             for g in range(group):
-                at = pl.multiple_of((n * group + g) * count, count)
+                at = pl.multiple_of((n * group + g) * 2 * count + h * count, count)
                 stage[pl.ds(at, count), :] = out[:, g * radial : (g + 1) * radial]
             return 0
 
-        lax.fori_loop(0, slab // group, planes_step, 0)
-
-        def turn(n, _):
+        lax.fori_loop(0, 2, half_step, 0)
+
+    def turn(into, f, first, begin, end):
+        def one(n, _):
             for u in range(8):
                 k = n * 8 + u
-                into[f, k] = stage[pl.ds(k, slab, stride=count), :].astype(jnp.bfloat16)
+                into[f, k] = stage[pl.ds(first + k, slab, stride=2 * count), :].astype(jnp.bfloat16)
             return 0
 
+        lax.fori_loop(begin // 8, end // 8, one, 0)
+
+    def give(f):
         for part in range(2):
-            lax.fori_loop(part * half // 8, (part + 1) * half // 8, turn, 0)
-            if first == 0:
-                twin_copy(f, part).start()
-
-    def give(f):
-        transform(f, given, 0)
+            if f == 2:
+                twin_copy(0, part).wait_send()
+            turn(given, f % 2, 0, part * half, (part + 1) * half)
+            twin_copy(f, part).start()
 
     def take(f):
-        transform(f, mine, count)
+        turn(mine, f, count, 0, count)
 
     def keep_copy(f, q):
-        at = pl.ds(q * step, step)
+        at = span_of(q)
         return pltpu.make_async_copy(mine.at[f, at], outs[f].at[at], keep_sem.at[f, q])
 
     def back_copy(f, q):
         return remote(
-            theirs.at[f, pl.ds(q * step, step)],
-            outs[f].at[pl.ds(count + q * step, step)],
+            theirs.at[f, span_of(q)],
+            outs[f].at[pl.ds(count + bounds[q] * fine, (bounds[q + 1] - bounds[q]) * fine)],
             back_send.at[f, q], back_recv.at[f, q], twin,
         )
 
@@ -553,8 +581,8 @@
         def one(n, _):
             found = []
             for u in range(16):
-                k = q * step + n * 16 + u
-                matrix = matrices[k]
+                k = bounds[q] * fine + n * 16 + u
+                matrix = jnp.concatenate([matrices[c, k] for c in range(chips)], axis=0)
                 for flip in (True, False):
                     chosen = [f for f in which if flips[f] == flip]
                     if not chosen:
@@ -574,7 +602,7 @@
                     theirs[f, k] = out[(2 * i + 1) * slab : (2 * i + 2) * slab]
             return 0
 
-        lax.fori_loop(0, step // 16, one, 0)
+        lax.fori_loop(0, (bounds[q + 1] - bounds[q]) * fine // 16, one, 0)
         for f in which:
             keep_copy(f, q).start()
             back_copy(f, q).start()
@@ -599,37 +627,43 @@
     tasks = {0: [begin], 1: [P(prepare, n) for n in range(4, strips)], 2: [table_in]}
     for n in range(strips):
         tasks.setdefault(2 + n, []).append(P(prepare, strips + n))
-    tasks |= {
-        13: [P(give, 0)],
-        14: [P(take, 0)],
-        16: [P(met, 0), P(solve, [0], 0), P(solve, [0], 1)],
-        17: [P(solve, [0], 2)],
-        18: [P(solve, [0], 3)],
-        21: [P(give, 1)],
-        22: [P(take, 1)],
-        24: [P(met, 1), P(solve, [1], 0), P(solve, [1], 1)],
-        25: [P(solve, [1], 2), P(solve, [1], 3)],
-        28: [P(solve, [0], 4), P(solve, [0], 7)],
-        29: [P(give, 2), P(take, 2), P(solve, [0], 5)],
-        30: [P(solve, [0], 6), P(met, 2)]
-        + [P(solve, [2], q) for q in range(early)]
-        + [P(solve, [1, 2], q) for q in (4, 7, 5, 6)],
+    for f in range(fields):
+        for n in range(slab // group):
+            ready = early + f * parts + (n + 1) * group // planes - 1
+            tasks.setdefault(ready, []).append(P(transform, f, n))
+    more = {
+        11: [P(give, 0), P(take, 0)],
+        13: [P(met, 0), P(solve, [0], 0)],
+        14: [P(solve, [0], 1)],
+        15: [P(solve, [0], 2)],
+        19: [P(give, 1), P(take, 1)],
+        21: [P(met, 1), P(solve, [1], 0)],
+        22: [P(solve, [1], 1), P(solve, [1], 2)],
+        24: [P(solve, [0, 1], 3)],
+        25: [P(solve, [0, 1], 4)],
+        26: [P(solve, [0, 1], 5)],
+        27: [P(give, 2), P(take, 2)],
+        28: [P(solve, [0, 1], 7), P(met, 2)] + [P(solve, [2], q) for q in (0, 1, 2, 3, 4, 5, 7)],
+        29: [P(solve, [0, 1, 2], 6)],
+        30: [P(solve, [0, 1, 2], 8)],
     }
+    for t, found in more.items():
+        tasks.setdefault(t, []).extend(found)
 
     shard_load.wait()
-    lag = 2
-    for t in range(31):
+    for t in range(ticks - 1):
         receive(t - lag)
         send(t)
         for task in tasks.get(t, []):
             task()
 
     edges_sent()
-    for t in range(31):
+    for t in range(ticks - 1):
         sent(t)
     for f in range(fields):
         for part in range(2):
-            twin_copy(f, part).wait_send()
+            if f > 0:
+                twin_copy(f, part).wait_send()
         for q in range(blocks):
             keep_copy(f, q).wait()
             back_copy(f, q).wait()
@@ -649,26 +683,26 @@
         in_specs=[pl.BlockSpec(memory_space=pl.ANY)] * 6,
         out_specs=[pl.BlockSpec(memory_space=pl.ANY)] * fields,
         scratch_shapes=[
-            pltpu.VMEM((count, radial, radial), jnp.bfloat16),
+            pltpu.VMEM((radial // rows, count, rows, radial), jnp.bfloat16),
             pltpu.VMEM((2 * count, 2 * local), jnp.bfloat16),
             pltpu.VMEM((fields, slab * radial, 2 * local), jnp.bfloat16),
-            pltpu.VMEM((slab * count, radial), jnp.float32),
+            pltpu.VMEM((2 * slab * count, radial), jnp.float32),
             modes,
             modes,
-            modes,
+            pltpu.VMEM((2, count, slab, radial), jnp.bfloat16),
             pltpu.VMEM((2, 2, slab + 2, strip, local), jnp.float32),
             pltpu.VMEM((2, 2, radial, local), jnp.float32),
             pltpu.VMEM((slab, local), jnp.int32),
             dma((blocks, 4)), dma((blocks, 4)),
-            dma((blocks + 1, 3)), dma((blocks + 1, 3)),
-            dma((blocks + 1, 3)), dma((blocks + 1, 3)),
-            dma((early + fields * blocks,)), dma((early + fields * blocks,)),
+            dma((blocks + len(crossed), 3)), dma((blocks + len(crossed), 3)),
+            dma((blocks + len(crossed), 3)), dma((blocks + len(crossed), 3)),
+            dma((early + fields * parts,)), dma((early + fields * parts,)),
             dma((fields, 2)), dma((fields, 2)),
             dma((fields, blocks)), dma((fields, blocks)), dma((fields, blocks)),
             dma((2,)), dma((4, 2)), dma((2, 6)), dma((2, 2)), dma((2, 2)),
         ],
         compiler_params=pltpu.CompilerParams(
-            collective_id=0, has_side_effects=True, vmem_limit_bytes=60 * 1024 * 1024
+            collective_id=0, has_side_effects=True, vmem_limit_bytes=62 * 1024 * 1024
         ),
         cost_estimate=pl.CostEstimate(flops=15 * 10**9, bytes_accessed=10**8, transcendentals=0),
     )(shard, table, cotangent, heat, tangent, wet)

time: 245 us -> 232 us (0.947)
  Pallas kernels: 216 us -> 204 us
    pallas_call x1, Pallas kernels: 208 us -> 197 us  [solved_modes(): pl.pallas_call(modes_kernel, out_shape=[out] * fields, in_specs=[pl.Block...]
where the time goes in v2:
time: 232 us
  Pallas kernels  204 us (88%)
  matrix products  14 us (6%)
  starting transfers between devices  5.69 us (2%)
  local copies, waits for them, and re-layouts  5.23 us (2%)
    pallas_call x1, Pallas kernels, solved_modes(): pl.pallas_call(modes_kernel, out_shape=[out] * fields, in_specs=[pl.Block...  197 us
    dot_general x3, matrix products, inverse(): jnp.einsum('ka,kzr->zra', to_azimuths, solved, preferred_element_type=jnp...  14 us
    pallas_call x1, Pallas kernels, by_radius(): pl.pallas_call(kernel, grid=(radial // rows,), in_specs=[pl.BlockSpec(wet...  7.71 us
  transfers between devices with their start and end apart: 3, of which 0 were waited for; matrix products, arithmetic and copies ran while one was open for 5% of the time, Pallas kernels for 0%

profile of v2, /device:TPU:1, one launch (start us, length us, event | category | flops | bytes accessed | tf_op | source)
XLA Modules:
  0.0 231.6 jit_solution(9370510177883340365)
XLA Ops:
  0.6 1.1 constant_dynamic-slice_fusion.4
  1.7 0.1 collective-permute-start
  1.8 1.7 constant_dynamic-slice_fusion
  3.6 0.0 copy-start.1
  3.6 0.1 fusion.20
  3.7 0.0 collective-permute-done
  3.7 1.1 copy-done.1
  4.8 0.1 broadcast_select_fusion.1
  4.9 1.2 pad_maximum_fusion.shard
  6.0 196.8 %shard_map.102 = (bf16[1024,16,128]{2,1,0:T(8,128)(2,1)}, bf16[1024,16,128]{2,1,0:T(8,128)(2,1)}, bf16[1024,16,128]{2,1,0:T(8,128)(2,1)}) custom-call(bf16[256,16,128]{2,1,0:T(8,128)(2,1)} %pad_maximum_fusion.shard, bf16[1024,1024]{1,0:T(8,128)(2,1)} %constant.27.clone.full, f32[16,128,512]{2,1,0:T(8,128)} %cotangent.1, f32[16,128,512]{2,1,0:T(8,128)} %heat.3, ...), custom_call_target="tpu_custom_call" | custom-call | flops 15000000512 | bytes 100000000 | tf_op jit(solution)/shard_map/pallas_call | solution.py:680
  202.8 0.0 copy-start.4
  202.8 0.0 copy-start.6
  202.9 5.0 %fusion.14.dual = bf16[16,128,512]{2,1,0:T(8,128)(2,1)S(1)} fusion(bf16[1024,512,1]{1,0,2:T(8,128)(2,1)S(1)} %fusion.20, bf16[1024,16,128]{2,1,0:T(8,128)(2,1)} %get-tuple-element.9), kind=kOutput, calls=%fused_computation.15 | convolution fusion | flops 2148532224 | bytes 7340032 | tf_op jit(solution)/shard_map/ka,kzr->zra/dot_general | solution.py:745
  207.8 0.0 copy-start
  207.8 2.1 collective-permute-start.2
  209.9 3.5 %collective-permute-start.1 = (bf16[1,128,512]{2,1,0:T(8,128)(2,1)S(1)}, bf16[1,128,512]{2,1,0:T(8,128)(2,1)S(1)}, u32[]{:S(2)}, u32[]{:S(2)}) collective-permute-start(bf16[1,128,512]{2,1,0:T(8,128)(2,1)S(1)} %get-tuple-element.11), channel_id=1, source_target_pairs={{0,2},{2,4},{4,6},{6,8},{8,10},{10,12},{12,14},{14,16},{16,18},{18... | collective-permute-start | bytes 393224 | tf_op jit(solution)/shard_map/ppermute | solution.py:22
  213.4 0.0 copy-done.4
  213.4 0.0 copy-done.6
  213.4 0.0 copy-start.5
  213.5 5.2 %fusion.7 = (bf16[16,512]{1,0:T(8,128)(2,1)}, bf16[16,128,512]{2,1,0:T(8,128)(2,1)}) fusion(s32[16,512]{1,0:T(8,128)S(1)} %copy-done.4, bf16[1024,512,1]{1,0,2:T(8,128)(2,1)S(1)} %fusion.20, bf16[1024,16,128]{2,1,0:T(8,128)(2,1)S(1)} %copy-done.6), kind=kOutput, calls=%fused_computation.8 | convolution fusion | flops 2151669760 | bytes 7389184 | tf_op jit(solution)/shard_map/ka,kzr->zra/dot_general | solution.py:745
  218.6 0.0 copy-done
  218.6 0.0 copy-done.5
  218.6 3.9 %fusion.11 = bf16[16,128,512]{2,1,0:T(8,128)(2,1)} fusion(bf16[1024,512,1]{1,0,2:T(8,128)(2,1)S(1)} %fusion.20, bf16[1024,16,128]{2,1,0:T(8,128)(2,1)S(1)} %copy-done.5), kind=kOutput, calls=%fused_computation.14 | convolution fusion | flops 2148532224 | bytes 7340032 | tf_op jit(solution)/shard_map/ka,kzr->zra/dot_general | solution.py:745
  222.6 0.0 collective-permute-done.2.dual_after
  222.6 0.0 copy-start.2
  222.6 0.0 collective-permute-done.1.dual_before
  222.6 0.6 copy-done.2
  223.2 0.0 copy-start.3
  223.2 0.6 copy-done.3
  223.9 7.7 %shard_map.103 = f32[16,128,512]{2,1,0:T(8,128)} custom-call(s32[16,512]{1,0:T(8,128)} %wet.3, f32[16,128,512]{2,1,0:T(8,128)} %heat.3, bf16[16,128,512]{2,1,0:T(8,128)(2,1)} %copy-done, bf16[1,128,512]{2,1,0:T(8,128)(2,1)} %copy-done.3, bf16[1,128,512]{2,1,0:T(8,128)(2,1)} %copy-done.2), custom_call_target="tpu_custom_call" | custom-call | flops 10485760 | bytes 6291456 | tf_op jit(solution)/shard_map/pallas_call | solution.py:75
  (1 shorter events, 0.0 us)
Async XLA Ops:
  1.7 2.0 collective-permute-start
  3.6 1.2 copy-start.1
  202.8 10.6 %copy-start.4 = (s32[16,512]{1,0:T(8,128)S(1)}, s32[16,512]{1,0:T(8,128)}, u32[]{:S(2)}) copy-start(s32[16,512]{1,0:T(8,128)} %param.11) | copy-start | bytes 98308
  202.8 10.6 %copy-start.6 = (bf16[1024,16,128]{2,1,0:T(8,128)(2,1)S(1)}, bf16[1024,16,128]{2,1,0:T(8,128)(2,1)}, u32[]{:S(2)}) copy-start(bf16[1024,16,128]{2,1,0:T(8,128)(2,1)} %get-tuple-element.7) | copy-start | bytes 12582916
  207.8 10.8 %copy-start = (bf16[16,128,512]{2,1,0:T(8,128)(2,1)}, bf16[16,128,512]{2,1,0:T(8,128)(2,1)S(1)}, u32[]{:S(2)}) copy-start(bf16[16,128,512]{2,1,0:T(8,128)(2,1)S(1)} %fusion.14.dual) | copy-start | bytes 6291460
  207.8 14.7 %collective-permute-start.2 = (bf16[1,128,512]{2,1,0:T(8,128)(2,1)S(1)}, bf16[1,128,512]{2,1,0:T(8,128)(2,1)S(1)}, u32[]{:S(2)}, u32[]{:S(2)}) collective-permute-start(bf16[1,128,512]{2,1,0:T(8,128)(2,1)S(1)} %get-tuple-element.10), channel_id=1, source_target_pairs={{2,0},{4,2},{6,4},{8,6},{10,8},{12,10},{14,12},{16,14},{18,16},{20... | collective-permute-start | bytes 393224 | tf_op jit(solution)/shard_map/ppermute | solution.py:23
  209.9 12.6 %collective-permute-start.1 = (bf16[1,128,512]{2,1,0:T(8,128)(2,1)S(1)}, bf16[1,128,512]{2,1,0:T(8,128)(2,1)S(1)}, u32[]{:S(2)}, u32[]{:S(2)}) collective-permute-start(bf16[1,128,512]{2,1,0:T(8,128)(2,1)S(1)} %get-tuple-element.11), channel_id=1, source_target_pairs={{0,2},{2,4},{4,6},{6,8},{8,10},{10,12},{12,14},{14,16},{16,18},{18... | collective-permute-start | bytes 393224 | tf_op jit(solution)/shard_map/ppermute | solution.py:22
  213.4 5.2 %copy-start.5 = (bf16[1024,16,128]{2,1,0:T(8,128)(2,1)S(1)}, bf16[1024,16,128]{2,1,0:T(8,128)(2,1)}, u32[]{:S(2)}) copy-start(bf16[1024,16,128]{2,1,0:T(8,128)(2,1)} %get-tuple-element.8) | copy-start | bytes 12582916
  222.6 0.6 copy-start.2
  223.2 0.6 copy-start.3

commit v3 on v2

--- a/solution.py
+++ b/solution.py
@@ -219,6 +219,7 @@
 blocks = len(bounds) - 1
 sections = ((0, 1, 2), (3, 4, 5), (6, 7, 8))
 crossed = (7, 8)
+order = (1, 2, 0)
 own, other = 0, 1
 ticks = 32
 
@@ -337,7 +338,8 @@
             mine_at = matrices.at[2 * z + x, pl.ds(n * step, step)]
             theirs_at = matrices.at[2 * z + x, pl.ds(half + n * step, step)]
             return remote(mine_at, theirs_at, azi_send.at[n], azi_recv.at[n], place, 1 - azi)
-        f, part = divmod(n - early, parts)
+        turn_of, part = divmod(n - early, parts)
+        f = order[turn_of]
         span = planes * radial
         at = pl.ds(part * span, span)
         return remote(
@@ -348,16 +350,23 @@
 
     pairs, lines, azis = pair_order(), line_order(), early + fields * parts
 
-    lag, lead = 2, 2
+    lag, lead = 2, 4
 
     def each(t, act):
         if 0 <= t < ticks:
             for item in pairs[t]:
                 act(pair_copy(*item))
 
+    def azi_until(t):
+        return early if t < 2 else min(t + lead + 1, azis)
+
     def azi_send_up_to(t):
-        for n in range(0 if t == 0 else t + lead, min(t + lead + 1, azis)):
+        for n in range(0 if t == 0 else azi_until(t - 1), azi_until(t)):
             azi_copy(n).start()
+
+    def azi_in(begin, end):
+        for n in range(begin, end):
+            azi_copy(n).wait_recv()
 
     def send(t):
         each(t, lambda copy: copy.start())
@@ -373,9 +382,8 @@
                 down_copy(q, c, p).start()
 
     def receive(t):
-        if t >= 0:
-            for n in range(0 if t == 0 else t + lead, min(t + lead + 1, azis)):
-                azi_copy(n).wait_recv()
+        if t == early:
+            azi_in(0, early)
         each(t, lambda copy: copy.wait_recv())
         for q, c, p in lines[t] if 0 <= t < ticks else ():
 
@@ -412,7 +420,7 @@
         slot = n % 2
         c = n % strips
         span = pl.ds(c * strip, strip)
-        if n < strips:
+        if n >= strips:
             return [
                 pltpu.make_async_copy(
                     cotangent.at[:, span, :], raw.at[slot, 0, pl.ds(1, slab)], raw_sem.at[slot, 0]
@@ -424,9 +432,6 @@
             found.append((edges.at[f, 0, span], raw.at[slot, f, 0], 3 * f + 1))
             found.append((edges.at[f, 1, span], raw.at[slot, f, slab + 1], 3 * f + 2))
         return [pltpu.make_async_copy(a, b, raw_sem.at[slot, i]) for a, b, i in found]
-
-    for load in strip_loads(0):
-        load.start()
 
     def edge_copies(side):
         out = []
@@ -491,8 +496,6 @@
     def prepare(n):
         slot = n % 2
         c = n % strips
-        if n + 1 == strips:
-            edges_in()
         if n + 1 < 2 * strips:
             for load in strip_loads(n + 1):
                 load.start()
@@ -503,7 +506,7 @@
 
         def plane_step(p, _):
             into = pl.ds(pl.multiple_of(p * radial + c * strip, strip), strip)
-            if n < strips:
+            if n >= strips:
                 values[0, into, pl.ds(0, local)] = raw[slot, 0, p + 1].astype(jnp.bfloat16)
                 return 0
             damping = damp[pl.ds(p, 1), :].astype(jnp.float32) * profile
@@ -526,7 +529,7 @@
     def twin_copy(f, part):
         at = pl.ds(part * half, half)
         return remote(
-            given.at[f % 2, at], theirs.at[f, at], twin_send.at[f, part], twin_recv.at[f, part], twin
+            given.at[order.index(f) % 2, at], theirs.at[f, at], twin_send.at[f, part], twin_recv.at[f, part], twin
         )
 
     group = 4
@@ -558,9 +561,9 @@
 
     def give(f):
         for part in range(2):
-            if f == 2:
-                twin_copy(0, part).wait_send()
-            turn(given, f % 2, 0, part * half, (part + 1) * half)
+            if f == order[2]:
+                twin_copy(order[0], part).wait_send()
+            turn(given, order.index(f) % 2, 0, part * half, (part + 1) * half)
             twin_copy(f, part).start()
 
     def take(f):
@@ -607,15 +610,17 @@
             keep_copy(f, q).start()
             back_copy(f, q).start()
 
-    def met(f):
-        for part in range(2):
-            twin_copy(f, part).wait_recv()
+    def met(f, part):
+        twin_copy(f, part).wait_recv()
 
     def begin():
         edges_out()
         for load in table_loads:
             load.start()
         damp_load.wait()
+        edges_in()
+        for load in strip_loads(0):
+            load.start()
         for n in range(4):
             prepare(n)
 
@@ -624,26 +629,36 @@
             load.wait()
 
     P = functools.partial
-    tasks = {0: [begin], 1: [P(prepare, n) for n in range(4, strips)], 2: [table_in]}
-    for n in range(strips):
-        tasks.setdefault(2 + n, []).append(P(prepare, strips + n))
-    for f in range(fields):
+    tasks = {
+        0: [begin],
+        1: [P(prepare, n) for n in range(4, strips)],
+        2: [P(prepare, n) for n in range(strips, strips + 4)],
+        4: [P(prepare, n) for n in range(strips + 4, 2 * strips)],
+        3: [table_in],
+    }
+    for turn_of, f in enumerate(order):
         for n in range(slab // group):
-            ready = early + f * parts + (n + 1) * group // planes - 1
-            tasks.setdefault(ready, []).append(P(transform, f, n))
+            begin = early + turn_of * parts + n * group // planes
+            end = begin + group // planes
+            ready = end - (2 if turn_of == 2 else 1)
+            tasks.setdefault(ready, []).append(P(azi_in, begin, end))
+            tasks[ready].append(P(transform, f, n))
     more = {
-        11: [P(give, 0), P(take, 0)],
-        13: [P(met, 0), P(solve, [0], 0)],
-        14: [P(solve, [0], 1)],
-        15: [P(solve, [0], 2)],
-        19: [P(give, 1), P(take, 1)],
-        21: [P(met, 1), P(solve, [1], 0)],
-        22: [P(solve, [1], 1), P(solve, [1], 2)],
-        24: [P(solve, [0, 1], 3)],
-        25: [P(solve, [0, 1], 4)],
-        26: [P(solve, [0, 1], 5)],
-        27: [P(give, 2), P(take, 2)],
-        28: [P(solve, [0, 1], 7), P(met, 2)] + [P(solve, [2], q) for q in (0, 1, 2, 3, 4, 5, 7)],
+        11: [P(give, 1), P(take, 1)],
+        13: [P(met, 1, 0), P(met, 1, 1), P(solve, [1], 0)],
+        14: [P(solve, [1], 1)],
+        15: [P(solve, [1], 2)],
+        19: [P(give, 2), P(take, 2)],
+        21: [P(met, 2, 0), P(met, 2, 1), P(solve, [2], 0)],
+        22: [P(solve, [2], 1), P(solve, [2], 2)],
+        24: [P(solve, [1, 2], 3)],
+        25: [P(solve, [1, 2], 4)],
+        26: [P(give, 0), P(take, 0)],
+        27: [P(solve, [1, 2], 5)],
+        28: [P(met, 0, 0)]
+        + [P(solve, [0], q) for q in range(4)]
+        + [P(solve, [1, 2], 7), P(met, 0, 1)]
+        + [P(solve, [0], q) for q in (4, 5, 7)],
         29: [P(solve, [0, 1, 2], 6)],
         30: [P(solve, [0, 1, 2], 8)],
     }
@@ -662,7 +677,7 @@
         sent(t)
     for f in range(fields):
         for part in range(2):
-            if f > 0:
+            if f != order[0]:
                 twin_copy(f, part).wait_send()
         for q in range(blocks):
             keep_copy(f, q).wait()
@@ -708,6 +723,29 @@
     )(shard, table, cotangent, heat, tangent, wet)
 
 
+def edged_gradient_kernel(wet, heat, dual, before, after, out):
+    rows = heat.shape[1]
+    at = pl.ds(pl.multiple_of(pl.program_id(0) * rows, rows), rows)
+    gradient_kernel(wet, heat, dual, before.at[:, at], after.at[:, at], out)
+
+
+def edged_gradient(wet, heat, dual, before, after):
+    slab, radial, lanes = heat.shape
+    rows = 32
+    spec = pl.BlockSpec((slab, rows, lanes), lambda i: (0, i, 0))
+    whole = pl.BlockSpec(memory_space=pltpu.VMEM)
+    return pl.pallas_call(
+        edged_gradient_kernel,
+        grid=(radial // rows,),
+        in_specs=[whole, spec, spec, whole, whole],
+        out_specs=spec,
+        out_shape=jax.ShapeDtypeStruct(heat.shape, jnp.float32),
+        cost_estimate=pl.CostEstimate(
+            flops=10 * heat.size, bytes_accessed=10 * heat.size, transcendentals=heat.size
+        ),
+    )(wet, heat, dual, before, after)
+
+
 def fused_body(table, heat_state, tangent_in, cotangent, wet_mask, sensors, propagators):
     slab, radial, local_azi = heat_state.shape
     depth = lax.axis_size("depth")
@@ -747,9 +785,7 @@
         ).astype(jnp.bfloat16)
 
     dual = inverse(dual_modes)
-    (gradient,) = by_radius(
-        gradient_kernel, wet_mask, [heat_state, dual, *halo_planes(dual[-1:], dual[:1])], [jnp.float32]
-    )
+    gradient = edged_gradient(wet_mask, heat_state, dual, *halo_planes(dual[-1:], dual[:1]))
     new_state = inverse(forward_modes)
     radial_index = jnp.arange(radial, dtype=jnp.int32)[None, :, None]
     selected = jnp.where(radial_index == sensors[:, None, :], new_state, jnp.zeros_like(new_state))

time: 232 us -> 229 us (0.987)
  Pallas kernels: 204 us -> 201 us
where the time goes in v3:
time: 229 us; the launch traced here: 228 us
  Pallas kernels  201 us (88%)
  matrix products  14 us (6%)
  starting transfers between devices  5.69 us (2%)
  local copies, waits for them, and re-layouts  5.23 us (2%)
    pallas_call x1, Pallas kernels, solved_modes(): pl.pallas_call(modes_kernel, out_shape=[out] * fields, in_specs=[pl.Block...  195 us
    dot_general x3, matrix products, inverse(): jnp.einsum('ka,kzr->zra', to_azimuths, solved, preferred_element_type=jnp...  14 us
    pallas_call x1, Pallas kernels, edged_gradient(): pl.pallas_call(edged_gradient_kernel, grid=(radial // rows,), in_specs=[w...  6.16 us
  transfers between devices with their start and end apart: 3, of which 0 were waited for; matrix products, arithmetic and copies ran while one was open for 5% of the time, Pallas kernels for 0%

profile of v3, /device:TPU:1, one launch (start us, length us, event | category | flops | bytes accessed | tf_op | source)
XLA Modules:
  0.0 228.3 jit_solution(16774474561240419186)
XLA Ops:
  0.6 1.1 constant_dynamic-slice_fusion.4
  1.7 0.1 collective-permute-start
  1.8 1.7 constant_dynamic-slice_fusion
  3.6 0.0 copy-start.1
  3.6 0.1 fusion.20
  3.7 0.0 collective-permute-done
  3.7 1.1 copy-done.1
  4.8 0.1 broadcast_select_fusion.1
  4.9 1.2 pad_maximum_fusion.shard
  6.0 195.0 %shard_map.102 = (bf16[1024,16,128]{2,1,0:T(8,128)(2,1)}, bf16[1024,16,128]{2,1,0:T(8,128)(2,1)}, bf16[1024,16,128]{2,1,0:T(8,128)(2,1)}) custom-call(bf16[256,16,128]{2,1,0:T(8,128)(2,1)} %pad_maximum_fusion.shard, bf16[1024,1024]{1,0:T(8,128)(2,1)} %constant.27.clone.full, f32[16,128,512]{2,1,0:T(8,128)} %cotangent.1, f32[16,128,512]{2,1,0:T(8,128)} %heat.3, ...), custom_call_target="tpu_custom_call" | custom-call | flops 15000000512 | bytes 100000000 | tf_op jit(solution)/shard_map/pallas_call | solution.py:695
  201.1 0.0 copy-start.4
  201.1 0.0 copy-start.6
  201.1 4.9 %fusion.14.dual = bf16[16,128,512]{2,1,0:T(8,128)(2,1)S(1)} fusion(bf16[1024,512,1]{1,0,2:T(8,128)(2,1)S(1)} %fusion.20, bf16[1024,16,128]{2,1,0:T(8,128)(2,1)} %get-tuple-element.9), kind=kOutput, calls=%fused_computation.15 | convolution fusion | flops 2148532224 | bytes 7340032 | tf_op jit(solution)/shard_map/ka,kzr->zra/dot_general | solution.py:783
  206.1 0.0 copy-start
  206.1 2.1 collective-permute-start.2
  208.2 3.5 %collective-permute-start.1 = (bf16[1,128,512]{2,1,0:T(8,128)(2,1)S(1)}, bf16[1,128,512]{2,1,0:T(8,128)(2,1)S(1)}, u32[]{:S(2)}, u32[]{:S(2)}) collective-permute-start(bf16[1,128,512]{2,1,0:T(8,128)(2,1)S(1)} %get-tuple-element.11), channel_id=1, source_target_pairs={{0,2},{2,4},{4,6},{6,8},{8,10},{10,12},{12,14},{14,16},{16,18},{18... | collective-permute-start | bytes 393224 | tf_op jit(solution)/shard_map/ppermute | solution.py:22
  211.7 0.0 copy-done.4
  211.7 0.0 copy-done.6
  211.7 0.0 copy-start.5
  211.7 5.2 %fusion.7 = (bf16[16,512]{1,0:T(8,128)(2,1)}, bf16[16,128,512]{2,1,0:T(8,128)(2,1)}) fusion(s32[16,512]{1,0:T(8,128)S(1)} %copy-done.4, bf16[1024,512,1]{1,0,2:T(8,128)(2,1)S(1)} %fusion.20, bf16[1024,16,128]{2,1,0:T(8,128)(2,1)S(1)} %copy-done.6), kind=kOutput, calls=%fused_computation.8 | convolution fusion | flops 2151669760 | bytes 7389184 | tf_op jit(solution)/shard_map/ka,kzr->zra/dot_general | solution.py:783
  216.9 0.0 copy-done
  216.9 0.0 copy-done.5
  216.9 3.9 %fusion.11 = bf16[16,128,512]{2,1,0:T(8,128)(2,1)} fusion(bf16[1024,512,1]{1,0,2:T(8,128)(2,1)S(1)} %fusion.20, bf16[1024,16,128]{2,1,0:T(8,128)(2,1)S(1)} %copy-done.5), kind=kOutput, calls=%fused_computation.14 | convolution fusion | flops 2148532224 | bytes 7340032 | tf_op jit(solution)/shard_map/ka,kzr->zra/dot_general | solution.py:783
  220.8 0.0 collective-permute-done.2.after
  220.8 0.0 copy-start.2
  220.8 0.0 collective-permute-done.1.before
  220.8 0.6 copy-done.2
  221.5 0.0 copy-start.3
  221.5 0.6 copy-done.3
  222.1 6.2 %shard_map.103 = f32[16,128,512]{2,1,0:T(8,128)} custom-call(s32[16,512]{1,0:T(8,128)} %wet.3, f32[16,128,512]{2,1,0:T(8,128)} %heat.3, bf16[16,128,512]{2,1,0:T(8,128)(2,1)} %copy-done, bf16[1,128,512]{2,1,0:T(8,128)(2,1)} %copy-done.3, bf16[1,128,512]{2,1,0:T(8,128)(2,1)} %copy-done.2), custom_call_target="tpu_custom_call" | custom-call | flops 10485760 | bytes 10485760 | tf_op jit(solution)/shard_map/pallas_call | solution.py:737
  (1 shorter events, 0.0 us)
Async XLA Ops:
  1.7 2.0 collective-permute-start
  3.6 1.2 copy-start.1
  201.1 10.6 %copy-start.4 = (s32[16,512]{1,0:T(8,128)S(1)}, s32[16,512]{1,0:T(8,128)}, u32[]{:S(2)}) copy-start(s32[16,512]{1,0:T(8,128)} %param.11) | copy-start | bytes 98308
  201.1 10.6 %copy-start.6 = (bf16[1024,16,128]{2,1,0:T(8,128)(2,1)S(1)}, bf16[1024,16,128]{2,1,0:T(8,128)(2,1)}, u32[]{:S(2)}) copy-start(bf16[1024,16,128]{2,1,0:T(8,128)(2,1)} %get-tuple-element.7) | copy-start | bytes 12582916
  206.1 10.8 %copy-start = (bf16[16,128,512]{2,1,0:T(8,128)(2,1)}, bf16[16,128,512]{2,1,0:T(8,128)(2,1)S(1)}, u32[]{:S(2)}) copy-start(bf16[16,128,512]{2,1,0:T(8,128)(2,1)S(1)} %fusion.14.dual) | copy-start | bytes 6291460
  206.1 14.7 %collective-permute-start.2 = (bf16[1,128,512]{2,1,0:T(8,128)(2,1)S(1)}, bf16[1,128,512]{2,1,0:T(8,128)(2,1)S(1)}, u32[]{:S(2)}, u32[]{:S(2)}) collective-permute-start(bf16[1,128,512]{2,1,0:T(8,128)(2,1)S(1)} %get-tuple-element.10), channel_id=1, source_target_pairs={{2,0},{4,2},{6,4},{8,6},{10,8},{12,10},{14,12},{16,14},{18,16},{20... | collective-permute-start | bytes 393224 | tf_op jit(solution)/shard_map/ppermute | solution.py:23
  208.2 12.7 %collective-permute-start.1 = (bf16[1,128,512]{2,1,0:T(8,128)(2,1)S(1)}, bf16[1,128,512]{2,1,0:T(8,128)(2,1)S(1)}, u32[]{:S(2)}, u32[]{:S(2)}) collective-permute-start(bf16[1,128,512]{2,1,0:T(8,128)(2,1)S(1)} %get-tuple-element.11), channel_id=1, source_target_pairs={{0,2},{2,4},{4,6},{6,8},{8,10},{10,12},{12,14},{14,16},{16,18},{18... | collective-permute-start | bytes 393224 | tf_op jit(solution)/shard_map/ppermute | solution.py:22
  211.7 5.2 %copy-start.5 = (bf16[1024,16,128]{2,1,0:T(8,128)(2,1)S(1)}, bf16[1024,16,128]{2,1,0:T(8,128)(2,1)}, u32[]{:S(2)}) copy-start(bf16[1024,16,128]{2,1,0:T(8,128)(2,1)} %get-tuple-element.8) | copy-start | bytes 12582916
  220.8 0.6 copy-start.2
  221.5 0.6 copy-start.3

commit v4 on v3

--- a/solution.py
+++ b/solution.py
@@ -252,9 +252,9 @@
 def modes_kernel(
     shard, full, cotangent, heat, tangent, wet,
     out_seed, out_forward, out_tangent,
-    matrices, table, values, stage, mine, theirs, given, raw, edges, damp,
+    matrices, table, values, stage, mine, theirs, given, raw, edges, edge_out, edge_in, damp,
     pair_send, pair_recv, up_send, up_recv, down_send, down_recv, azi_send, azi_recv,
-    twin_send, twin_recv, back_send, back_recv, keep_sem, load_sem, table_sem, raw_sem, edge_send, edge_recv,
+    twin_send, twin_recv, back_send, back_recv, keep_sem, load_sem, table_sem, raw_sem, edge_load, edge_send, edge_recv,
 ):
     outs = (out_seed, out_forward, out_tangent)
     flips = (True, False, False)
@@ -435,17 +435,31 @@
 
     def edge_copies(side):
         out = []
-        for f, source in enumerate((heat, tangent)):
+        for f in range(2):
             out.append(
                 remote(
-                    source.at[slab - 1 if side == 0 else 0], edges.at[f, side],
+                    edge_out.at[f, side], edge_in.at[f, side],
                     edge_send.at[f, side], edge_recv.at[f, side],
                     place + 1 if side == 0 else place - 1,
                 )
             )
         return out
 
+    edge_loads = [
+        pltpu.make_async_copy(
+            source.at[slab - 1 if side == 0 else 0], edges.at[f, side], edge_load.at[f, side]
+        )
+        for f, source in enumerate((heat, tangent))
+        for side in range(2)
+    ]
+
     def edges_out():
+        for load in edge_loads:
+            load.start()
+        for load in edge_loads:
+            load.wait()
+        edge_out[...] = edges[...].astype(jnp.bfloat16)
+
         @pl.when(place < last)
         def _():
             for copy in edge_copies(0):
@@ -463,6 +477,7 @@
             def _():
                 for copy in edge_copies(side):
                     copy.wait_recv()
+                edges[:, side] = edge_in[:, side].astype(jnp.float32)
 
             @pl.when(empty)
             def _():
@@ -653,12 +668,9 @@
         22: [P(solve, [2], 1), P(solve, [2], 2)],
         24: [P(solve, [1, 2], 3)],
         25: [P(solve, [1, 2], 4)],
-        26: [P(give, 0), P(take, 0)],
-        27: [P(solve, [1, 2], 5)],
-        28: [P(met, 0, 0)]
-        + [P(solve, [0], q) for q in range(4)]
-        + [P(solve, [1, 2], 7), P(met, 0, 1)]
-        + [P(solve, [0], q) for q in (4, 5, 7)],
+        26: [P(give, 0), P(take, 0), P(solve, [1, 2], 5)],
+        27: [P(met, 0, 0)] + [P(solve, [0], q) for q in range(4)],
+        28: [P(solve, [1, 2], 7), P(met, 0, 1)] + [P(solve, [0], q) for q in (4, 5, 7)],
         29: [P(solve, [0, 1, 2], 6)],
         30: [P(solve, [0, 1, 2], 8)],
     }
@@ -707,6 +719,8 @@
             pltpu.VMEM((2, count, slab, radial), jnp.bfloat16),
             pltpu.VMEM((2, 2, slab + 2, strip, local), jnp.float32),
             pltpu.VMEM((2, 2, radial, local), jnp.float32),
+            pltpu.VMEM((2, 2, radial, local), jnp.bfloat16),
+            pltpu.VMEM((2, 2, radial, local), jnp.bfloat16),
             pltpu.VMEM((slab, local), jnp.int32),
             dma((blocks, 4)), dma((blocks, 4)),
             dma((blocks + len(crossed), 3)), dma((blocks + len(crossed), 3)),
@@ -714,7 +728,7 @@
             dma((early + fields * parts,)), dma((early + fields * parts,)),
             dma((fields, 2)), dma((fields, 2)),
             dma((fields, blocks)), dma((fields, blocks)), dma((fields, blocks)),
-            dma((2,)), dma((4, 2)), dma((2, 6)), dma((2, 2)), dma((2, 2)),
+            dma((2,)), dma((4, 2)), dma((2, 6)), dma((2, 2)), dma((2, 2)), dma((2, 2)),
         ],
         compiler_params=pltpu.CompilerParams(
             collective_id=0, has_side_effects=True, vmem_limit_bytes=62 * 1024 * 1024
@@ -757,9 +771,9 @@
     mine = lax.dynamic_slice_in_dim(propagators, core * half, half, axis=0)
     outgoing = lax.dynamic_slice_in_dim(propagators, (1 - core) * half, half, axis=0)
     incoming = lax.ppermute(outgoing, "depth", [(i, i ^ 1) for i in range(depth)])
-    shard = jnp.concatenate(
-        [jnp.where(core == 0, mine, incoming), jnp.where(core == 0, incoming, mine)], axis=1
-    )
+    rows = mine.shape[1]
+    at_core = lax.broadcasted_iota(jnp.int32, (1, 2, 1, 1), 1) == core
+    shard = jnp.where(at_core, mine[:, None], incoming[:, None]).reshape(half, 2 * rows, radial)
 
     def table_rows(which):
         return [

time: 229 us -> 222 us (0.969)
  Pallas kernels: 201 us -> 196 us
    pallas_call x1, Pallas kernels: 195 us -> 189 us  [solved_modes(): pl.pallas_call(modes_kernel, out_shape=[out] * fields, in_specs=[pl.Block...]
where the time goes in v4:
time: 222 us
  Pallas kernels  196 us (88%)
  matrix products  14 us (6%)
  starting transfers between devices  5.69 us (3%)
  local copies, waits for them, and re-layouts  4.49 us (2%)
    pallas_call x1, Pallas kernels, solved_modes(): pl.pallas_call(modes_kernel, out_shape=[out] * fields, in_specs=[pl.Block...  189 us
    dot_general x3, matrix products, inverse(): jnp.einsum('ka,kzr->zra', to_azimuths, solved, preferred_element_type=jnp...  14 us
    pallas_call x1, Pallas kernels, edged_gradient(): pl.pallas_call(edged_gradient_kernel, grid=(radial // rows,), in_specs=[w...  6.16 us
  transfers between devices with their start and end apart: 3, of which 0 were waited for; matrix products, arithmetic and copies ran while one was open for 5% of the time, Pallas kernels for 0%

profile of v4, /device:TPU:1, one launch (start us, length us, event | category | flops | bytes accessed | tf_op | source)
XLA Modules:
  0.0 221.8 jit_solution(4062205734063973385)
XLA Ops:
  0.6 1.3 constant_dynamic-slice_fusion.5
  1.9 0.1 collective-permute-start
  2.1 0.1 broadcast_in_dim.39
  2.1 0.1 broadcast_in_dim.40
  2.2 1.7 constant_dynamic-slice_fusion
  4.0 0.1 fusion.20
  4.1 0.0 collective-permute-done
  4.1 1.2 bitcast_select_fusion.shard
  5.2 189.4 %shard_map.102 = (bf16[1024,16,128]{2,1,0:T(8,128)(2,1)}, bf16[1024,16,128]{2,1,0:T(8,128)(2,1)}, bf16[1024,16,128]{2,1,0:T(8,128)(2,1)}) custom-call(bf16[256,16,128]{2,1,0:T(8,128)(2,1)} %bitcast_select_fusion.shard, bf16[1024,1024]{1,0:T(8,128)(2,1)} %constant.27.clone.full, f32[16,128,512]{2,1,0:T(8,128)} %cotangent.1, f32[16,128,512]{2,1,0:T(8,128)} %heat.3, ...), custom_call_target="tpu_custom_call" | custom-call | flops 15000000512 | bytes 100000000 | tf_op jit(solution)/shard_map/pallas_call | solution.py:707
  194.6 0.0 copy-start.3
  194.6 0.0 copy-start.5
  194.6 5.0 %fusion.14.dual = bf16[16,128,512]{2,1,0:T(8,128)(2,1)S(1)} fusion(bf16[1024,512,1]{1,0,2:T(8,128)(2,1)S(1)} %fusion.20, bf16[1024,16,128]{2,1,0:T(8,128)(2,1)} %get-tuple-element.9), kind=kOutput, calls=%fused_computation.15 | convolution fusion | flops 2148532224 | bytes 7340032 | tf_op jit(solution)/shard_map/ka,kzr->zra/dot_general | solution.py:797
  199.6 0.0 copy-start
  199.6 2.0 collective-permute-start.2
  201.7 3.5 %collective-permute-start.1 = (bf16[1,128,512]{2,1,0:T(8,128)(2,1)S(1)}, bf16[1,128,512]{2,1,0:T(8,128)(2,1)S(1)}, u32[]{:S(2)}, u32[]{:S(2)}) collective-permute-start(bf16[1,128,512]{2,1,0:T(8,128)(2,1)S(1)} %get-tuple-element.11), channel_id=1, source_target_pairs={{0,2},{2,4},{4,6},{6,8},{8,10},{10,12},{12,14},{14,16},{16,18},{18... | collective-permute-start | bytes 393224 | tf_op jit(solution)/shard_map/ppermute | solution.py:22
  205.2 0.0 copy-done.3
  205.2 0.0 copy-done.5
  205.2 0.0 copy-start.4
  205.2 5.2 %fusion.7 = (bf16[16,512]{1,0:T(8,128)(2,1)}, bf16[16,128,512]{2,1,0:T(8,128)(2,1)}) fusion(s32[16,512]{1,0:T(8,128)S(1)} %copy-done.3, bf16[1024,512,1]{1,0,2:T(8,128)(2,1)S(1)} %fusion.20, bf16[1024,16,128]{2,1,0:T(8,128)(2,1)S(1)} %copy-done.5), kind=kOutput, calls=%fused_computation.8 | convolution fusion | flops 2151669760 | bytes 7389184 | tf_op jit(solution)/shard_map/ka,kzr->zra/dot_general | solution.py:797
  210.4 0.0 copy-done
  210.4 0.0 copy-done.4
  210.4 3.9 %fusion.11 = bf16[16,128,512]{2,1,0:T(8,128)(2,1)} fusion(bf16[1024,512,1]{1,0,2:T(8,128)(2,1)S(1)} %fusion.20, bf16[1024,16,128]{2,1,0:T(8,128)(2,1)S(1)} %copy-done.4), kind=kOutput, calls=%fused_computation.14 | convolution fusion | flops 2148532224 | bytes 7340032 | tf_op jit(solution)/shard_map/ka,kzr->zra/dot_general | solution.py:797
  214.3 0.0 collective-permute-done.2.after
  214.3 0.0 copy-start.1
  214.3 0.0 collective-permute-done.1.before
  214.3 0.6 copy-done.1
  215.0 0.0 copy-start.2
  215.0 0.6 copy-done.2
  215.6 6.2 %shard_map.103 = f32[16,128,512]{2,1,0:T(8,128)} custom-call(s32[16,512]{1,0:T(8,128)} %wet.3, f32[16,128,512]{2,1,0:T(8,128)} %heat.3, bf16[16,128,512]{2,1,0:T(8,128)(2,1)} %copy-done, bf16[1,128,512]{2,1,0:T(8,128)(2,1)} %copy-done.2, bf16[1,128,512]{2,1,0:T(8,128)(2,1)} %copy-done.1), custom_call_target="tpu_custom_call" | custom-call | flops 10485760 | bytes 10485760 | tf_op jit(solution)/shard_map/pallas_call | solution.py:751
  (2 shorter events, 0.0 us)
Async XLA Ops:
  1.9 2.2 collective-permute-start
  194.6 10.6 %copy-start.3 = (s32[16,512]{1,0:T(8,128)S(1)}, s32[16,512]{1,0:T(8,128)}, u32[]{:S(2)}) copy-start(s32[16,512]{1,0:T(8,128)} %param.11) | copy-start | bytes 98308
  194.6 10.6 %copy-start.5 = (bf16[1024,16,128]{2,1,0:T(8,128)(2,1)S(1)}, bf16[1024,16,128]{2,1,0:T(8,128)(2,1)}, u32[]{:S(2)}) copy-start(bf16[1024,16,128]{2,1,0:T(8,128)(2,1)} %get-tuple-element.7) | copy-start | bytes 12582916
  199.6 10.8 %copy-start = (bf16[16,128,512]{2,1,0:T(8,128)(2,1)}, bf16[16,128,512]{2,1,0:T(8,128)(2,1)S(1)}, u32[]{:S(2)}) copy-start(bf16[16,128,512]{2,1,0:T(8,128)(2,1)S(1)} %fusion.14.dual) | copy-start | bytes 6291460
  199.6 14.7 %collective-permute-start.2 = (bf16[1,128,512]{2,1,0:T(8,128)(2,1)S(1)}, bf16[1,128,512]{2,1,0:T(8,128)(2,1)S(1)}, u32[]{:S(2)}, u32[]{:S(2)}) collective-permute-start(bf16[1,128,512]{2,1,0:T(8,128)(2,1)S(1)} %get-tuple-element.10), channel_id=1, source_target_pairs={{2,0},{4,2},{6,4},{8,6},{10,8},{12,10},{14,12},{16,14},{18,16},{20... | collective-permute-start | bytes 393224 | tf_op jit(solution)/shard_map/ppermute | solution.py:23
  201.7 12.7 %collective-permute-start.1 = (bf16[1,128,512]{2,1,0:T(8,128)(2,1)S(1)}, bf16[1,128,512]{2,1,0:T(8,128)(2,1)S(1)}, u32[]{:S(2)}, u32[]{:S(2)}) collective-permute-start(bf16[1,128,512]{2,1,0:T(8,128)(2,1)S(1)} %get-tuple-element.11), channel_id=1, source_target_pairs={{0,2},{2,4},{4,6},{6,8},{8,10},{10,12},{12,14},{14,16},{16,18},{18... | collective-permute-start | bytes 393224 | tf_op jit(solution)/shard_map/ppermute | solution.py:22
  205.2 5.2 %copy-start.4 = (bf16[1024,16,128]{2,1,0:T(8,128)(2,1)S(1)}, bf16[1024,16,128]{2,1,0:T(8,128)(2,1)}, u32[]{:S(2)}) copy-start(bf16[1024,16,128]{2,1,0:T(8,128)(2,1)} %get-tuple-element.8) | copy-start | bytes 12582916
  214.3 0.7 copy-start.1
  215.0 0.6 copy-start.2

commit v5 on v4

--- a/solution.py
+++ b/solution.py
@@ -598,8 +598,8 @@
     def solve(which, q):
         def one(n, _):
             found = []
-            for u in range(16):
-                k = bounds[q] * fine + n * 16 + u
+            for u in range(32):
+                k = bounds[q] * fine + n * 32 + u
                 matrix = jnp.concatenate([matrices[c, k] for c in range(chips)], axis=0)
                 for flip in (True, False):
                     chosen = [f for f in which if flips[f] == flip]
@@ -620,7 +620,7 @@
                     theirs[f, k] = out[(2 * i + 1) * slab : (2 * i + 2) * slab]
             return 0
 
-        lax.fori_loop(0, (bounds[q + 1] - bounds[q]) * fine // 16, one, 0)
+        lax.fori_loop(0, (bounds[q + 1] - bounds[q]) * fine // 32, one, 0)
         for f in which:
             keep_copy(f, q).start()
             back_copy(f, q).start()

time: 222 us -> 220 us (level)
  Pallas kernels: 196 us -> 193 us
where the time goes in v5:
time: 220 us
  Pallas kernels  193 us (88%)
  matrix products  14 us (6%)
  starting transfers between devices  5.69 us (3%)
  local copies, waits for them, and re-layouts  4.49 us (2%)
    pallas_call x1, Pallas kernels, solved_modes(): pl.pallas_call(modes_kernel, out_shape=[out] * fields, in_specs=[pl.Block...  187 us
    dot_general x3, matrix products, inverse(): jnp.einsum('ka,kzr->zra', to_azimuths, solved, preferred_element_type=jnp...  14 us
    pallas_call x1, Pallas kernels, edged_gradient(): pl.pallas_call(edged_gradient_kernel, grid=(radial // rows,), in_specs=[w...  6.16 us
  transfers between devices with their start and end apart: 3, of which 0 were waited for; matrix products, arithmetic and copies ran while one was open for 5% of the time, Pallas kernels for 0%

profile of v5, /device:TPU:1, one launch (start us, length us, event | category | flops | bytes accessed | tf_op | source)
XLA Modules:
  0.0 219.6 jit_solution(9119552569857729248)
XLA Ops:
  0.6 1.3 constant_dynamic-slice_fusion.5
  1.9 0.1 collective-permute-start
  2.1 0.1 broadcast_in_dim.39
  2.1 0.1 broadcast_in_dim.40
  2.2 1.7 constant_dynamic-slice_fusion
  4.0 0.1 fusion.20
  4.1 0.0 collective-permute-done
  4.1 1.2 bitcast_select_fusion.shard
  5.2 187.2 %shard_map.102 = (bf16[1024,16,128]{2,1,0:T(8,128)(2,1)}, bf16[1024,16,128]{2,1,0:T(8,128)(2,1)}, bf16[1024,16,128]{2,1,0:T(8,128)(2,1)}) custom-call(bf16[256,16,128]{2,1,0:T(8,128)(2,1)} %bitcast_select_fusion.shard, bf16[1024,1024]{1,0:T(8,128)(2,1)} %constant.27.clone.full, f32[16,128,512]{2,1,0:T(8,128)} %cotangent.1, f32[16,128,512]{2,1,0:T(8,128)} %heat.3, ...), custom_call_target="tpu_custom_call" | custom-call | flops 15000000512 | bytes 100000000 | tf_op jit(solution)/shard_map/pallas_call | solution.py:707
  192.4 0.0 copy-start.3
  192.4 0.0 copy-start.5
  192.4 4.9 %fusion.14.dual = bf16[16,128,512]{2,1,0:T(8,128)(2,1)S(1)} fusion(bf16[1024,512,1]{1,0,2:T(8,128)(2,1)S(1)} %fusion.20, bf16[1024,16,128]{2,1,0:T(8,128)(2,1)} %get-tuple-element.9), kind=kOutput, calls=%fused_computation.15 | convolution fusion | flops 2148532224 | bytes 7340032 | tf_op jit(solution)/shard_map/ka,kzr->zra/dot_general | solution.py:797
  197.4 0.0 copy-start
  197.4 2.1 collective-permute-start.2
  199.5 3.5 %collective-permute-start.1 = (bf16[1,128,512]{2,1,0:T(8,128)(2,1)S(1)}, bf16[1,128,512]{2,1,0:T(8,128)(2,1)S(1)}, u32[]{:S(2)}, u32[]{:S(2)}) collective-permute-start(bf16[1,128,512]{2,1,0:T(8,128)(2,1)S(1)} %get-tuple-element.11), channel_id=1, source_target_pairs={{0,2},{2,4},{4,6},{6,8},{8,10},{10,12},{12,14},{14,16},{16,18},{18... | collective-permute-start | bytes 393224 | tf_op jit(solution)/shard_map/ppermute | solution.py:22
  203.0 0.0 copy-done.3
  203.0 0.0 copy-done.5
  203.0 0.0 copy-start.4
  203.0 5.2 %fusion.7 = (bf16[16,512]{1,0:T(8,128)(2,1)}, bf16[16,128,512]{2,1,0:T(8,128)(2,1)}) fusion(s32[16,512]{1,0:T(8,128)S(1)} %copy-done.3, bf16[1024,512,1]{1,0,2:T(8,128)(2,1)S(1)} %fusion.20, bf16[1024,16,128]{2,1,0:T(8,128)(2,1)S(1)} %copy-done.5), kind=kOutput, calls=%fused_computation.8 | convolution fusion | flops 2151669760 | bytes 7389184 | tf_op jit(solution)/shard_map/ka,kzr->zra/dot_general | solution.py:797
  208.2 0.0 copy-done
  208.2 0.0 copy-done.4
  208.2 3.9 %fusion.11 = bf16[16,128,512]{2,1,0:T(8,128)(2,1)} fusion(bf16[1024,512,1]{1,0,2:T(8,128)(2,1)S(1)} %fusion.20, bf16[1024,16,128]{2,1,0:T(8,128)(2,1)S(1)} %copy-done.4), kind=kOutput, calls=%fused_computation.14 | convolution fusion | flops 2148532224 | bytes 7340032 | tf_op jit(solution)/shard_map/ka,kzr->zra/dot_general | solution.py:797
  212.1 0.0 collective-permute-done.2.after
  212.1 0.0 copy-start.1
  212.1 0.0 collective-permute-done.1.before
  212.1 0.6 copy-done.1
  212.8 0.0 copy-start.2
  212.8 0.6 copy-done.2
  213.4 6.2 %shard_map.103 = f32[16,128,512]{2,1,0:T(8,128)} custom-call(s32[16,512]{1,0:T(8,128)} %wet.3, f32[16,128,512]{2,1,0:T(8,128)} %heat.3, bf16[16,128,512]{2,1,0:T(8,128)(2,1)} %copy-done, bf16[1,128,512]{2,1,0:T(8,128)(2,1)} %copy-done.2, bf16[1,128,512]{2,1,0:T(8,128)(2,1)} %copy-done.1), custom_call_target="tpu_custom_call" | custom-call | flops 10485760 | bytes 10485760 | tf_op jit(solution)/shard_map/pallas_call | solution.py:751
  (2 shorter events, 0.0 us)
Async XLA Ops:
  1.9 2.2 collective-permute-start
  192.4 10.6 %copy-start.3 = (s32[16,512]{1,0:T(8,128)S(1)}, s32[16,512]{1,0:T(8,128)}, u32[]{:S(2)}) copy-start(s32[16,512]{1,0:T(8,128)} %param.11) | copy-start | bytes 98308
  192.4 10.6 %copy-start.5 = (bf16[1024,16,128]{2,1,0:T(8,128)(2,1)S(1)}, bf16[1024,16,128]{2,1,0:T(8,128)(2,1)}, u32[]{:S(2)}) copy-start(bf16[1024,16,128]{2,1,0:T(8,128)(2,1)} %get-tuple-element.7) | copy-start | bytes 12582916
  197.4 10.8 %copy-start = (bf16[16,128,512]{2,1,0:T(8,128)(2,1)}, bf16[16,128,512]{2,1,0:T(8,128)(2,1)S(1)}, u32[]{:S(2)}) copy-start(bf16[16,128,512]{2,1,0:T(8,128)(2,1)S(1)} %fusion.14.dual) | copy-start | bytes 6291460
  197.4 14.7 %collective-permute-start.2 = (bf16[1,128,512]{2,1,0:T(8,128)(2,1)S(1)}, bf16[1,128,512]{2,1,0:T(8,128)(2,1)S(1)}, u32[]{:S(2)}, u32[]{:S(2)}) collective-permute-start(bf16[1,128,512]{2,1,0:T(8,128)(2,1)S(1)} %get-tuple-element.10), channel_id=1, source_target_pairs={{2,0},{4,2},{6,4},{8,6},{10,8},{12,10},{14,12},{16,14},{18,16},{20... | collective-permute-start | bytes 393224 | tf_op jit(solution)/shard_map/ppermute | solution.py:23
  199.5 12.7 %collective-permute-start.1 = (bf16[1,128,512]{2,1,0:T(8,128)(2,1)S(1)}, bf16[1,128,512]{2,1,0:T(8,128)(2,1)S(1)}, u32[]{:S(2)}, u32[]{:S(2)}) collective-permute-start(bf16[1,128,512]{2,1,0:T(8,128)(2,1)S(1)} %get-tuple-element.11), channel_id=1, source_target_pairs={{0,2},{2,4},{4,6},{6,8},{8,10},{10,12},{12,14},{14,16},{16,18},{18... | collective-permute-start | bytes 393224 | tf_op jit(solution)/shard_map/ppermute | solution.py:22
  203.0 5.2 %copy-start.4 = (bf16[1024,16,128]{2,1,0:T(8,128)(2,1)S(1)}, bf16[1024,16,128]{2,1,0:T(8,128)(2,1)}, u32[]{:S(2)}) copy-start(bf16[1024,16,128]{2,1,0:T(8,128)(2,1)} %get-tuple-element.8) | copy-start | bytes 12582916
  212.1 0.7 copy-start.1
  212.8 0.6 copy-start.2
